TPU v7x, 32 devices: a whole 2x2x4 slice. The times are simulated.
32 devices in a mesh: gx: 8 (over y, x, core), ch: 4 (over z).
Axes of the slice: x: 2, y: 2, z: 4, core: 2. Of those that a mesh axis runs over, the one named last changes fastest.
Arguments:
- activations: bfloat16 [128, 128, 4, 128], P('ch', 'gx'), may hold values from -6 to 6
- conv_weight: bfloat16 [27, 128, 128], P(None, None, 'ch'), may hold values from -0.109375 to 0.109375
- out_grad: bfloat16 [128, 128, 4, 128], P('ch', 'gx'), may hold values from -6 to 6
Outputs:
- features_out: bfloat16 [128, 128, 4, 128], P('ch', 'gx')
- input_grad: bfloat16 [128, 128, 4, 128], P('ch', 'gx')
All inputs are finite; a program needn't handle non-finite values.
Results may differ from a plain program's by a relative error of at most 0.001.
Values may be sent and summed in bfloat16 or wider, within the bound.
A program may use at most 64 MiB of HBM per device.

v0:
```python
import jax
import jax.numpy as jnp
from jax import lax
from jax.sharding import PartitionSpec as P


def with_halo(cells, sides, width):
    for axis, dim in sides:
        count = lax.axis_size(axis)
        head = lax.slice_in_dim(cells, 0, width, axis=dim)
        tail = lax.slice_in_dim(cells, cells.shape[dim] - width, cells.shape[dim], axis=dim)
        cells = jnp.concatenate(
            [
                lax.ppermute(tail, axis, [(i, (i + 1) % count) for i in range(count)]),
                cells,
                lax.ppermute(head, axis, [((i + 1) % count, i) for i in range(count)]),
            ],
            axis=dim,
        )
    return cells


def tap_sum(extended, weight, direction, pattern):
    planes = extended.shape[1] - 2
    depth = extended.shape[2]
    height = extended.shape[3]
    padded = jnp.pad(extended, ((0, 0), (0, 0), (1, 1), (1, 1)))
    summed = None
    for first in range(3):
        for second in range(3):
            for third in range(3):
                offset_x = 1 + direction * (first - 1)
                offset_y = 1 + direction * (second - 1)
                offset_z = 1 + direction * (third - 1)
                window_part = padded[
                    :,
                    offset_x : offset_x + planes,
                    offset_z : offset_z + depth,
                    offset_y : offset_y + height,
                ]
                product = jnp.einsum(
                    pattern,
                    window_part,
                    weight[9 * first + 3 * second + third],
                    preferred_element_type=jnp.float32,
                )
                summed = product if summed is None else summed + product
    return summed


def cell_faces(field):
    return with_halo(field, ((("gx", "ch"), 1),), 1)


def local(activations, conv_weight, out_grad):
    full_weight = lax.all_gather(conv_weight, "ch", axis=2, tiled=True)
    cells_act, cells_grad = (
        lax.all_to_all(activations, "ch", split_axis=1, concat_axis=0, tiled=True),
        lax.all_to_all(out_grad, "ch", split_axis=1, concat_axis=0, tiled=True),
    )
    forward = tap_sum(cell_faces(cells_act), full_weight, 1, "kxzy,kn->nxzy").astype(jnp.bfloat16)
    backward = tap_sum(cell_faces(cells_grad), full_weight, -1, "kxzy,nk->nxzy").astype(
        jnp.bfloat16
    )
    features_out, input_grad = (
        lax.all_to_all(forward, "ch", split_axis=0, concat_axis=1, tiled=True),
        lax.all_to_all(backward, "ch", split_axis=0, concat_axis=1, tiled=True),
    )
    return (features_out, input_grad)


def solution(mesh):
    return jax.shard_map(
        local,
        mesh=mesh,
        in_specs=(P("ch", "gx", None, None), P(None, None, "ch"), P("ch", "gx", None, None)),
        out_specs=(P("ch", "gx", None, None), P("ch", "gx", None, None)),
        check_vma=False,
    )
```

profile of v0, /device:TPU:0, one launch (start us, length us, event | category | flops | bytes accessed | tf_op | source)
XLA Modules:
  0.0 145.1 jit_solution(14141572523261221364)
XLA Ops:
  0.6 2.2 %copy.92 = bf16[32,16,4,128]{3,0,2,1:T(8,128)(2,1)} copy(bf16[32,16,4,128]{3,2,1,0:T(4,128)(2,1)} %param.5) | data formatting | bytes 1048576 | tf_op args[2]
  2.9 6.3 %all-to-all-start.2 = ((bf16[32,16,4,128]{3,0,2,1:T(8,128)(2,1)}), bf16[32,16,4,128]{3,0,2,1:T(8,128)(2,1)S(1)}, u32[]{:S(2)}, u32[]{:S(2)}) async-start(bf16[32,16,4,128]{3,0,2,1:T(8,128)(2,1)} %copy.92), calls=%async_computation.2 | async-start | bytes 1048576 | tf_op jit(solution)/shard_map/all_to_all | solution.py:59
  10.3 13.3 %all-to-all-done.2 = bf16[32,16,4,128]{3,0,2,1:T(8,128)(2,1)S(1)} async-done(((bf16[32,16,4,128]{3,0,2,1:T(8,128)(2,1)}), bf16[32,16,4,128]{3,0,2,1:T(8,128)(2,1)S(1)}, u32[]{:S(2)}, u32[]{:S(2)}) %all-to-all-start.2) | async-done | bytes 524320 | tf_op jit(solution)/shard_map/all_to_all | solution.py:59
  23.7 3.5 %all-to-all-start = ((bf16[32,16,4,128]{3,0,2,1:T(8,128)(2,1)}), bf16[32,16,4,128]{3,0,2,1:T(8,128)(2,1)S(1)}, u32[]{:S(2)}, u32[]{:S(2)}) async-start(bf16[32,16,4,128]{3,0,2,1:T(8,128)(2,1)} %copy.55), calls=%async_computation | async-start | bytes 1048576 | tf_op jit(solution)/shard_map/all_to_all | solution.py:58
  27.2 28.7 %all_gather.3 = bf16[27,128,128]{1,2,0:T(8,128)(2,1)S(1)} all-gather(bf16[27,128,32]{1,2,0:T(8,128)(2,1)S(1)} %copy-done.16), channel_id=1, replica_groups=mesh['gx'=8,'ch'=4] {'ch'}, dimensions={2}, use_global_device_ids=true | all-gather | bytes 1105920 | tf_op jit(solution)/shard_map/all_gather | solution.py:56
  56.2 1.3 fusion.130
  57.9 1.3 fusion.131
  60.2 4.5 %collective-permute-start.3 = (bf16[128,1,4,128]{0,3,2,1:T(8,128)(2,1)S(1)}, bf16[128,1,4,128]{0,3,2,1:T(8,128)(2,1)S(1)}, u32[]{:S(2)}, u32[]{:S(2)}) collective-permute-start(bf16[128,1,4,128]{0,3,2,1:T(8,128)(2,1)S(1)} %get-tuple-element.7), channel_id=1, source_target_pairs={{1,0},{2,1},{3,2},{4,3},{5,4},{6,5},{7,6},{8,7},{9,8},{10,9},{11,1... | collective-permute-start | bytes 393224 | tf_op jit(solution)/shard_map/ppermute | solution.py:16
  64.8 5.3 %collective-permute-start.1 = (bf16[128,1,4,128]{0,3,2,1:T(8,128)(2,1)S(1)}, bf16[128,1,4,128]{0,3,2,1:T(8,128)(2,1)S(1)}, u32[]{:S(2)}, u32[]{:S(2)}) collective-permute-start(bf16[128,1,4,128]{0,3,2,1:T(8,128)(2,1)S(1)} %get-tuple-element.9), channel_id=1, source_target_pairs={{1,0},{2,1},{3,2},{4,3},{5,4},{6,5},{7,6},{8,7},{9,8},{10,9},{11,1... | collective-permute-start | bytes 393224 | tf_op jit(solution)/shard_map/ppermute | solution.py:16
  80.4 1.4 convolution_bitcast_fusion.23
  81.8 1.4 fusion.109
  84.5 1.3 fusion.113
  88.4 1.3 fusion.119
  89.7 1.3 fusion.121
  93.6 1.3 convolution_bitcast_fusion.17
  94.9 1.3 convolution_bitcast_fusion.18
  98.8 1.3 convolution_bitcast_fusion.13
  105.7 2.2 %copy.101 = bf16[128,4,4,128]{3,2,1,0:T(4,128)(2,1)} copy(bf16[128,4,4,128]{0,3,2,1:T(8,128)(2,1)} %fusion.50) | data formatting | bytes 1048576 | tf_op jit(solution)/shard_map/convert_element_type | solution.py:62
  107.9 4.4 %all-to-all-start.3 = ((bf16[128,4,4,128]{3,2,1,0:T(4,128)(2,1)}), bf16[128,4,4,128]{3,2,1,0:T(4,128)(2,1)}, u32[]{:S(2)}, u32[]{:S(2)}) async-start(bf16[128,4,4,128]{3,2,1,0:T(4,128)(2,1)} %copy.101), calls=%async_computation.3 | async-start | bytes 1048576 | tf_op jit(solution)/shard_map/all_to_all | solution.py:67
  112.3 1.7 %convolution_add_fusion.7 = f32[4,4,128,128]{3,2,1,0:T(8,128)S(1)} fusion(f32[4,4,128,128]{3,2,1,0:T(8,128)} %fusion.128, bf16[128,6,6,130]{0,3,2,1:T(8,128)(2,1)S(1)} %select_maximum_fusion.2, bf16[27,128,128]{1,2,0:T(8,128)(2,1)S(1)} %all_gather.3), kind=kOutput, calls=%fused_computation.82 | convolution fusion | flops 67371008 | bytes 2654208 | tf_op jit(solution)/shard_map/kxzy,kn->nxzy/dot_general | solution.py:41
  116.5 3.4 %fusion.48 = f32[128,4,4,128]{0,3,2,1:T(8,128)S(1)} fusion(f32[128,4,4,128]{0,3,2,1:T(8,128)S(1)} %copy-done.9, f32[128,4,4,128]{0,3,2,1:T(8,128)S(1)} %copy-done.10, f32[128,4,4,128]{0,3,2,1:T(8,128)S(1)} %copy-done.11, f32[128,4,4,128]{0,3,2,1:T(8,128)S(1)} %copy-done.7, f32[4,4,128,128]{3,2,1,0:T(8,128)S(1)} %copy-done.12, ...), kind=kOutput, calls=%fused_computation.86 | convolution fusion | flops 71827456 | bytes 15368192 | tf_op jit(solution)/shard_map/kxzy,kn->nxzy/dot_general | solution.py:41
  124.6 1.8 %all-to-all-done.3 = bf16[128,4,4,128]{3,2,1,0:T(4,128)(2,1)} async-done(((bf16[128,4,4,128]{3,2,1,0:T(4,128)(2,1)}), bf16[128,4,4,128]{3,2,1,0:T(4,128)(2,1)}, u32[]{:S(2)}, u32[]{:S(2)}) %all-to-all-start.3) | async-done | bytes 524320 | tf_op jit(solution)/shard_map/all_to_all | solution.py:67
  126.4 3.5 %all-to-all-start.1 = ((bf16[128,4,4,128]{3,2,1,0:T(4,128)(2,1)}), bf16[128,4,4,128]{3,2,1,0:T(4,128)(2,1)S(1)}, u32[]{:S(2)}, u32[]{:S(2)}) async-start(bf16[128,4,4,128]{3,2,1,0:T(4,128)(2,1)} %copy.89), calls=%async_computation.1 | async-start | bytes 1048576 | tf_op jit(solution)/shard_map/all_to_all | solution.py:66
  132.2 11.6 %all-to-all-done.1 = bf16[128,4,4,128]{3,2,1,0:T(4,128)(2,1)S(1)} async-done(((bf16[128,4,4,128]{3,2,1,0:T(4,128)(2,1)}), bf16[128,4,4,128]{3,2,1,0:T(4,128)(2,1)S(1)}, u32[]{:S(2)}, u32[]{:S(2)}) %all-to-all-start.1) | async-done | bytes 524320 | tf_op jit(solution)/shard_map/all_to_all | solution.py:66
  (99 shorter events, 38.2 us)
Async XLA Ops:
  0.6 8.6 %copy-start.15 = (bf16[32,16,4,128]{3,2,1,0:T(4,128)(2,1)S(1)}, bf16[32,16,4,128]{3,2,1,0:T(4,128)(2,1)}, u32[]{:S(2)}) copy-start(bf16[32,16,4,128]{3,2,1,0:T(4,128)(2,1)} %param.3) | copy-start | bytes 1572868
  2.9 20.8 %all-to-all-start.2 = ((bf16[32,16,4,128]{3,0,2,1:T(8,128)(2,1)}), bf16[32,16,4,128]{3,0,2,1:T(8,128)(2,1)S(1)}, u32[]{:S(2)}, u32[]{:S(2)}) async-start(bf16[32,16,4,128]{3,0,2,1:T(8,128)(2,1)} %copy.92), calls=%async_computation.2 | async-start | bytes 1048576 | tf_op jit(solution)/shard_map/all_to_all | solution.py:59
  9.2 18.0 %copy-start.16 = (bf16[27,128,32]{1,2,0:T(8,128)(2,1)S(1)}, bf16[27,128,32]{1,2,0:T(8,128)(2,1)}, u32[]{:S(2)}) copy-start(bf16[27,128,32]{1,2,0:T(8,128)(2,1)} %param.4) | copy-start | bytes 663556
  23.7 33.9 %all-to-all-start = ((bf16[32,16,4,128]{3,0,2,1:T(8,128)(2,1)}), bf16[32,16,4,128]{3,0,2,1:T(8,128)(2,1)S(1)}, u32[]{:S(2)}, u32[]{:S(2)}) async-start(bf16[32,16,4,128]{3,0,2,1:T(8,128)(2,1)} %copy.55), calls=%async_computation | async-start | bytes 1048576 | tf_op jit(solution)/shard_map/all_to_all | solution.py:58
  59.3 10.8 %collective-permute-start.2 = (bf16[128,1,4,128]{0,3,2,1:T(8,128)(2,1)S(1)}, bf16[128,1,4,128]{0,3,2,1:T(8,128)(2,1)S(1)}, u32[]{:S(2)}, u32[]{:S(2)}) collective-permute-start(bf16[128,1,4,128]{0,3,2,1:T(8,128)(2,1)S(1)} %get-tuple-element.6), channel_id=1, source_target_pairs={{0,1},{1,2},{2,3},{3,4},{4,5},{5,6},{6,7},{7,8},{8,9},{9,10},{10,1... | collective-permute-start | bytes 393224 | tf_op jit(solution)/shard_map/ppermute | solution.py:14
  60.2 10.0 %collective-permute-start.3 = (bf16[128,1,4,128]{0,3,2,1:T(8,128)(2,1)S(1)}, bf16[128,1,4,128]{0,3,2,1:T(8,128)(2,1)S(1)}, u32[]{:S(2)}, u32[]{:S(2)}) collective-permute-start(bf16[128,1,4,128]{0,3,2,1:T(8,128)(2,1)S(1)} %get-tuple-element.7), channel_id=1, source_target_pairs={{1,0},{2,1},{3,2},{4,3},{5,4},{6,5},{7,6},{8,7},{9,8},{10,9},{11,1... | collective-permute-start | bytes 393224 | tf_op jit(solution)/shard_map/ppermute | solution.py:16
  64.7 11.6 %collective-permute-start = (bf16[128,1,4,128]{0,3,2,1:T(8,128)(2,1)S(1)}, bf16[128,1,4,128]{0,3,2,1:T(8,128)(2,1)S(1)}, u32[]{:S(2)}, u32[]{:S(2)}) collective-permute-start(bf16[128,1,4,128]{0,3,2,1:T(8,128)(2,1)S(1)} %get-tuple-element.8), channel_id=1, source_target_pairs={{0,1},{1,2},{2,3},{3,4},{4,5},{5,6},{6,7},{7,8},{8,9},{9,10},{10,1... | collective-permute-start | bytes 393224 | tf_op jit(solution)/shard_map/ppermute | solution.py:14
  64.8 11.5 %collective-permute-start.1 = (bf16[128,1,4,128]{0,3,2,1:T(8,128)(2,1)S(1)}, bf16[128,1,4,128]{0,3,2,1:T(8,128)(2,1)S(1)}, u32[]{:S(2)}, u32[]{:S(2)}) collective-permute-start(bf16[128,1,4,128]{0,3,2,1:T(8,128)(2,1)S(1)} %get-tuple-element.9), channel_id=1, source_target_pairs={{1,0},{2,1},{3,2},{4,3},{5,4},{6,5},{7,6},{8,7},{9,8},{10,9},{11,1... | collective-permute-start | bytes 393224 | tf_op jit(solution)/shard_map/ppermute | solution.py:16
  102.0 1.2 copy-start.8
  107.9 18.5 %all-to-all-start.3 = ((bf16[128,4,4,128]{3,2,1,0:T(4,128)(2,1)}), bf16[128,4,4,128]{3,2,1,0:T(4,128)(2,1)}, u32[]{:S(2)}, u32[]{:S(2)}) async-start(bf16[128,4,4,128]{3,2,1,0:T(4,128)(2,1)} %copy.101), calls=%async_computation.3 | async-start | bytes 1048576 | tf_op jit(solution)/shard_map/all_to_all | solution.py:67
  112.2 2.4 %copy-start.13 = (f32[4,4,128,128]{3,2,1,0:T(8,128)S(1)}, f32[4,4,128,128]{3,2,1,0:T(8,128)}, u32[]{:S(2)}) copy-start(f32[4,4,128,128]{3,2,1,0:T(8,128)} %fusion.111) | copy-start | bytes 3145732
  112.3 2.4 %copy-start.14 = (f32[4,4,128,128]{3,2,1,0:T(8,128)S(1)}, f32[4,4,128,128]{3,2,1,0:T(8,128)}, u32[]{:S(2)}) copy-start(f32[4,4,128,128]{3,2,1,0:T(8,128)} %fusion.113) | copy-start | bytes 3145732
  113.9 1.3 copy-start.10
  113.9 1.6 %copy-start.11 = (f32[128,4,4,128]{0,3,2,1:T(8,128)S(1)}, f32[128,4,4,128]{0,3,2,1:T(8,128)}, u32[]{:S(2)}) copy-start(f32[128,4,4,128]{0,3,2,1:T(8,128)} %convolution_bitcast_fusion.23) | copy-start | bytes 3145732
  114.0 1.9 %copy-start.12 = (f32[4,4,128,128]{3,2,1,0:T(8,128)S(1)}, f32[4,4,128,128]{3,2,1,0:T(8,128)}, u32[]{:S(2)}) copy-start(f32[4,4,128,128]{3,2,1,0:T(8,128)} %fusion.109) | copy-start | bytes 3145732
  114.3 1.9 %copy-start.7 = (f32[128,4,4,128]{0,3,2,1:T(8,128)S(1)}, f32[128,4,4,128]{0,3,2,1:T(8,128)}, u32[]{:S(2)}) copy-start(f32[128,4,4,128]{0,3,2,1:T(8,128)} %fusion.131) | copy-start | bytes 3145732
  114.3 2.2 %copy-start.9 = (f32[128,4,4,128]{0,3,2,1:T(8,128)S(1)}, f32[128,4,4,128]{0,3,2,1:T(8,128)}, u32[]{:S(2)}) copy-start(f32[128,4,4,128]{0,3,2,1:T(8,128)} %convolution_bitcast_fusion.21) | copy-start | bytes 3145732
  116.5 3.7 %copy-start.4 = (f32[128,4,4,128]{0,3,2,1:T(8,128)S(1)}, f32[128,4,4,128]{0,3,2,1:T(8,128)}, u32[]{:S(2)}) copy-start(f32[128,4,4,128]{0,3,2,1:T(8,128)} %convolution_bitcast_fusion.17) | copy-start | bytes 3145732
  116.5 3.7 %copy-start.5 = (f32[128,4,4,128]{0,3,2,1:T(8,128)S(1)}, f32[128,4,4,128]{0,3,2,1:T(8,128)}, u32[]{:S(2)}) copy-start(f32[128,4,4,128]{0,3,2,1:T(8,128)} %convolution_bitcast_fusion.18) | copy-start | bytes 3145732
  116.5 3.8 %copy-start.6 = (f32[128,4,4,128]{0,3,2,1:T(8,128)S(1)}, f32[128,4,4,128]{0,3,2,1:T(8,128)}, u32[]{:S(2)}) copy-start(f32[128,4,4,128]{0,3,2,1:T(8,128)} %convolution_bitcast_fusion.19) | copy-start | bytes 3145732
  119.9 1.2 copy-start.3
  121.1 1.5 %copy-start.1 = (f32[128,4,4,128]{0,3,2,1:T(8,128)S(1)}, f32[128,4,4,128]{0,3,2,1:T(8,128)}, u32[]{:S(2)}) copy-start(f32[128,4,4,128]{0,3,2,1:T(8,128)} %convolution_bitcast_fusion.13) | copy-start | bytes 3145732
  121.1 1.9 %copy-start.2 = (f32[128,4,4,128]{0,3,2,1:T(8,128)S(1)}, f32[128,4,4,128]{0,3,2,1:T(8,128)}, u32[]{:S(2)}) copy-start(f32[128,4,4,128]{0,3,2,1:T(8,128)} %convolution_bitcast_fusion.14) | copy-start | bytes 3145732
  126.4 17.4 %all-to-all-start.1 = ((bf16[128,4,4,128]{3,2,1,0:T(4,128)(2,1)}), bf16[128,4,4,128]{3,2,1,0:T(4,128)(2,1)S(1)}, u32[]{:S(2)}, u32[]{:S(2)}) async-start(bf16[128,4,4,128]{3,2,1,0:T(4,128)(2,1)} %copy.89), calls=%async_computation.1 | async-start | bytes 1048576 | tf_op jit(solution)/shard_map/all_to_all | solution.py:66
  (1 other events, 1.2 us)
where the time goes:
time: 146 us; the launch traced here: 145 us
  matrix products  43.5 us (30%)
  blocking collectives  28.7 us (20%)
  starting transfers between devices  28.4 us (19%)
  waiting for transfers between devices  26.8 us (18%)
  local copies, waits for them, and re-layouts  16.1 us (11%)
    dot_general x54, matrix products, tap_sum(): jnp.einsum(pattern, window_part, weight[9 * first + 3 * second + third],...  43.5 us
    all_gather x1, blocking collectives, local(): full_weight = lax.all_gather(conv_weight, 'ch', axis=2, tiled=True)  28.7 us
    all_to_all x1, waiting for transfers between devices, local(): lax.all_to_all(out_grad, 'ch', split_axis=1, concat_axis=0, tiled=True)  13.3 us
    all_to_all x1, waiting for transfers between devices, local(): lax.all_to_all(forward, 'ch', split_axis=0, concat_axis=1, tiled=True)  11.6 us
    unnamed x38, local copies, waits for them, and re-layouts  10.5 us
    ppermute x2, starting transfers between devices, with_halo(): lax.ppermute(head, axis, [((i + 1) % count, i) for i in range(count)])  9.87 us
    all_to_all x1, starting transfers between devices, local(): lax.all_to_all(out_grad, 'ch', split_axis=1, concat_axis=0, tiled=True)  6.32 us
    all_to_all x1, starting transfers between devices, local(): lax.all_to_all(backward, 'ch', split_axis=0, concat_axis=1, tiled=True)  4.35 us
  transfers between devices with their start and end apart: 8, of which 3 were waited for; matrix products, arithmetic and copies ran while one was open for 13% of the time, Pallas kernels for 0%

commit v1 on v0

--- a/solution.py
+++ b/solution.py
@@ -1,7 +1,13 @@
+import functools
+
 import jax
 import jax.numpy as jnp
 from jax import lax
+from jax.experimental import pallas as pl
+from jax.experimental.pallas import tpu as pltpu
 from jax.sharding import PartitionSpec as P
+
+MESH = pl.DeviceIdType.MESH
 
 
 def with_halo(cells, sides, width):
@@ -52,7 +58,7 @@
     return with_halo(field, ((("gx", "ch"), 1),), 1)
 
 
-def local(activations, conv_weight, out_grad):
+def local_plain(activations, conv_weight, out_grad):
     full_weight = lax.all_gather(conv_weight, "ch", axis=2, tiled=True)
     cells_act, cells_grad = (
         lax.all_to_all(activations, "ch", split_axis=1, concat_axis=0, tiled=True),
@@ -62,11 +68,254 @@
     backward = tap_sum(cell_faces(cells_grad), full_weight, -1, "kxzy,nk->nxzy").astype(
         jnp.bfloat16
     )
-    features_out, input_grad = (
+    return (
         lax.all_to_all(forward, "ch", split_axis=0, concat_axis=1, tiled=True),
         lax.all_to_all(backward, "ch", split_axis=0, concat_axis=1, tiled=True),
     )
-    return (features_out, input_grad)
+
+
+def kernel(
+    dims, act, grad, wsl, outf, outg,
+    xa, xg, gathered, lf, lb, yf, yg,
+    w1_send, w1_recv, w2_send, w2_recv, in_send, in_recv, halo_send, halo_recv,
+    out_send, out_recv, own,
+):
+    n, m, rows, block, depth, height, taps = dims
+    chans = m * rows
+    per = wsl.shape[0]
+    plane = depth * height
+    span = block * plane
+    g = lax.axis_index("gx")
+    d = lax.axis_index("ch")
+
+    def block_of(gg, dd):
+        return jnp.where(lax.rem(gg, 2) == 0, dd, m - 1 - dd)
+
+    k = block_of(g, d)
+
+    def device_of(index):
+        gg = lax.div(index, m)
+        return gg, block_of(gg, lax.rem(index, m))
+
+    whole = n * m
+    spot = g * m + k
+    prev = device_of(lax.rem(spot + whole - 1, whole))
+    following = device_of(lax.rem(spot + 1, whole))
+
+    def rows_at(dd):
+        return pl.ds(pl.multiple_of(dd * rows, rows), rows)
+
+    def cols_at(kk):
+        return pl.ds(pl.multiple_of(kk * span, 128), span)
+
+    barrier = pltpu.get_barrier_semaphore()
+    for r in range(1, m):
+        pl.semaphore_signal(barrier, inc=1, device_id=(g, lax.rem(d + r, m)), device_id_type=MESH)
+    for r in range(1, n):
+        pl.semaphore_signal(barrier, inc=1, device_id=(lax.rem(g + r, n), d), device_id_type=MESH)
+    pl.semaphore_wait(barrier, m - 1 + n - 1)
+
+    def remote(src, dst, send, recv, where):
+        return pltpu.make_async_remote_copy(
+            src_ref=src, dst_ref=dst, send_sem=send, recv_sem=recv,
+            device_id=where, device_id_type=MESH,
+        )
+
+    mine = pl.ds(g * per, per)
+
+    def w1(r, sending):
+        dd = lax.rem(d + r, m) if sending else lax.rem(d + m - r, m)
+        at = d if sending else dd
+        return remote(wsl, gathered.at[mine, rows_at(at), :], w1_send.at[r], w1_recv.at[r], (g, dd))
+
+    def w2(r, sending):
+        gg = lax.rem(g + r, n) if sending else lax.rem(g + n - r, n)
+        at = g if sending else gg
+        part = gathered.at[pl.ds(at * per, per), :, :]
+        return remote(part, part, w2_send.at[r], w2_recv.at[r], (gg, d))
+
+    def spread(which, x, field, r, sending):
+        dd = lax.rem(d + r, m) if sending else lax.rem(d + m - r, m)
+        at = d if sending else dd
+        return remote(
+            field.at[:, cols_at(block_of(g, dd) if sending else k)],
+            x.at[rows_at(at), pl.ds(plane, span)],
+            in_send.at[which, r], in_recv.at[which, r], (g, dd),
+        )
+
+    def halo(which, x, side):
+        first, last = pl.ds(plane, plane), pl.ds(span, plane)
+        low, high = pl.ds(0, plane), pl.ds(span + plane, plane)
+        src, dst, where = ((first, high, prev), (last, low, following))[side]
+        return remote(
+            x.at[:, src], x.at[:, dst], halo_send.at[which, side], halo_recv.at[which, side], where
+        )
+
+    def collect(which, y, out, r, sending):
+        dd = lax.rem(d + r, m) if sending else lax.rem(d + m - r, m)
+        at = k if sending else block_of(g, dd)
+        return remote(
+            y.at[rows_at(dd if sending else d), :], out.at[:, cols_at(at)],
+            out_send.at[which, r], out_recv.at[which, r], (g, dd),
+        )
+
+    own_copies = [
+        pltpu.make_async_copy(wsl, gathered.at[mine, rows_at(d), :], own.at[0]),
+        pltpu.make_async_copy(act.at[:, cols_at(k)], xa.at[rows_at(d), pl.ds(plane, span)], own.at[1]),
+        pltpu.make_async_copy(grad.at[:, cols_at(k)], xg.at[rows_at(d), pl.ds(plane, span)], own.at[2]),
+    ]
+    others, peers = range(1, m), range(1, n)
+    for r in others:
+        w1(r, True).start()
+    for r in others:
+        spread(0, xa, act, r, True).start()
+    for c in own_copies:
+        c.start()
+    for c in own_copies:
+        c.wait()
+    for r in others:
+        w1(r, False).wait_recv()
+
+    @pl.when(g * per < taps)
+    def _():
+        for r in peers:
+            w2(r, True).start()
+
+    for r in others:
+        spread(0, xa, act, r, True).wait_send()
+    for r in others:
+        spread(1, xg, grad, r, True).start()
+    for r in others:
+        spread(0, xa, act, r, False).wait_recv()
+    for side in range(2):
+        halo(0, xa, side).start()
+
+    for r in peers:
+        @pl.when(lax.rem(g + n - r, n) * per < taps)
+        def _():
+            w2(r, False).wait_recv()
+
+    for a in range(3):
+        for b in range(3):
+            for c in range(3):
+                at = pl.ds((3 * c + a) * chans, chans)
+                lf[pl.ds(b * chans, chans), at] = gathered[9 * a + 3 * b + c]
+                lb[pl.ds(b * chans, chans), at] = gathered[9 * (2 - a) + 3 * (2 - b) + 2 - c].T
+
+    lane = lax.broadcasted_iota(jnp.int32, (chans, height), 1)
+
+    def pair_sum(x, l, y, pair):
+        def cells(slot, z):
+            return x[:, pl.ds(slot * plane + z * height, height)]
+
+        for z in range(depth):
+            inside = [c for c in range(3) if 0 <= z + c - 1 < depth]
+            right = jnp.concatenate(
+                [
+                    jnp.concatenate([cells(s + a - 1, z + c - 1) for s in pair], axis=1)
+                    for c in inside
+                    for a in range(3)
+                ],
+                axis=0,
+            )
+            left = l[:, pl.ds(inside[0] * 3 * chans, len(inside) * 3 * chans)]
+            acc = jnp.dot(left, right, preferred_element_type=jnp.float32)
+            for i, s in enumerate(pair):
+                part = acc[:, i * height : (i + 1) * height]
+                below = pltpu.roll(part[:chans], 1, 1)
+                above = pltpu.roll(part[2 * chans :], height - 1, 1)
+                total = (
+                    part[chans : 2 * chans]
+                    + jnp.where(lane > 0, below, 0.0)
+                    + jnp.where(lane < height - 1, above, 0.0)
+                )
+                y[:, pl.ds((s - 1) * plane + z * height, height)] = total.astype(y.dtype)
+
+    def finish(which, x, l, y, out):
+        for s in range(2, block, 2):
+            pair_sum(x, l, y, (s, s + 1))
+        for side in range(2):
+            halo(which, x, side).wait_recv()
+        pair_sum(x, l, y, (1, block))
+        for r in others:
+            collect(which, y, out, r, True).start()
+        copy = pltpu.make_async_copy(y.at[rows_at(d), :], out.at[:, cols_at(k)], own.at[3 + which])
+        copy.start()
+        return copy
+
+    first_own = finish(0, xa, lf, yf, outf)
+    for r in others:
+        spread(1, xg, grad, r, False).wait_recv()
+    for side in range(2):
+        halo(1, xg, side).start()
+    second_own = finish(1, xg, lb, yg, outg)
+
+    first_own.wait()
+    second_own.wait()
+    for r in others:
+        collect(0, yf, outf, r, False).wait_recv()
+        collect(1, yg, outg, r, False).wait_recv()
+        w1(r, True).wait_send()
+        spread(1, xg, grad, r, True).wait_send()
+        collect(0, yf, outf, r, True).wait_send()
+        collect(1, yg, outg, r, True).wait_send()
+    for which, x in ((0, xa), (1, xg)):
+        for side in range(2):
+            halo(which, x, side).wait_send()
+
+    @pl.when(g * per < taps)
+    def _():
+        for r in peers:
+            w2(r, True).wait_send()
+
+
+def local_kernel(activations, conv_weight, out_grad):
+    n, m = lax.axis_size("gx"), lax.axis_size("ch")
+    rows, planes, depth, height = activations.shape
+    taps, chans, _ = conv_weight.shape
+    block = planes // m
+    plane = depth * height
+    per = -(-taps // n)
+    padded = jnp.pad(conv_weight, ((0, per * n - taps), (0, 0), (0, 0)))
+    wsl = lax.dynamic_slice_in_dim(padded, lax.axis_index("gx") * per, per, axis=0)
+    wsl = jnp.swapaxes(wsl, 1, 2)
+    vmem = pl.BlockSpec(memory_space=pltpu.VMEM)
+    flat = jax.ShapeDtypeStruct((rows, planes * plane), jnp.bfloat16)
+    sem = pltpu.SemaphoreType.DMA
+    flops = 2 * 2 * taps * chans * chans * block * plane
+    features, gradient = pl.pallas_call(
+        functools.partial(kernel, (n, m, rows, block, depth, height, taps)),
+        out_shape=(flat, flat),
+        in_specs=[vmem] * 3,
+        out_specs=(vmem, vmem),
+        scratch_shapes=[
+            pltpu.VMEM((chans, (block + 2) * plane), jnp.bfloat16),
+            pltpu.VMEM((chans, (block + 2) * plane), jnp.bfloat16),
+            pltpu.VMEM((per * n, chans, chans), jnp.bfloat16),
+            pltpu.VMEM((3 * chans, 9 * chans), jnp.bfloat16),
+            pltpu.VMEM((3 * chans, 9 * chans), jnp.bfloat16),
+            pltpu.VMEM((chans, block * plane), jnp.bfloat16),
+            pltpu.VMEM((chans, block * plane), jnp.bfloat16),
+            sem((m,)), sem((m,)), sem((n,)), sem((n,)),
+            sem((2, m)), sem((2, m)), sem((2, 2)), sem((2, 2)),
+            sem((2, m)), sem((2, m)), sem((5,)),
+        ],
+        compiler_params=pltpu.CompilerParams(
+            collective_id=0, has_side_effects=True, vmem_limit_bytes=40 * 2**20
+        ),
+        cost_estimate=pl.CostEstimate(
+            flops=flops, bytes_accessed=8 * rows * planes * plane, transcendentals=0
+        ),
+    )(activations.reshape(rows, -1), out_grad.reshape(rows, -1), wsl)
+    return features.reshape(activations.shape), gradient.reshape(out_grad.shape)
+
+
+def local(activations, conv_weight, out_grad):
+    n, m = lax.axis_size("gx"), lax.axis_size("ch")
+    rows, planes, _, height = activations.shape
+    fits = rows % 16 == 0 and planes % (2 * m) == 0 and height % 128 == 0 and n % 2 == 0
+    plan = local_kernel if fits else local_plain
+    return plan(activations, conv_weight, out_grad)
 
 
 def solution(mesh):

time: 146 us -> 68.5 us (0.47)
  Pallas kernels: 0 us -> 62.7 us
  matrix products: 43.5 us -> 0 us
  blocking collectives: 28.7 us -> 0 us
  starting transfers between devices: 28.4 us -> 0 us
  waiting for transfers between devices: 26.8 us -> 0 us
  local copies, waits for them, and re-layouts: 16.1 us -> 4.97 us
    pallas_call x0 -> x1, Pallas kernels: none -> 62.7 us  [local_kernel(): pl.pallas_call(functools.partial(kernel, (n, m, rows, block, depth, heigh...]
    dot_general x54 -> x0, matrix products: 43.5 us -> none  [tap_sum(): jnp.einsum(pattern, window_part, weight[9 * first + 3 * second + third],...]
    all_gather x1 -> x0, blocking collectives: 28.7 us -> none  [local(): full_weight = lax.all_gather(conv_weight, 'ch', axis=2, tiled=True)]
    all_to_all x4 -> x0, waiting for transfers between devices: 26.8 us -> none  [the longest x1 13.3 us: local(): lax.all_to_all(out_grad, 'ch', split_axis=1, concat_axis=0, tiled=True)]
    all_to_all x4 -> x0, starting transfers between devices: 17.6 us -> none  [the longest x1 6.32 us: local(): lax.all_to_all(out_grad, 'ch', split_axis=1, concat_axis=0, tiled=True)]
    ppermute x4 -> x0, starting transfers between devices: 10.8 us -> none  [the longest x2 9.87 us: with_halo(): lax.ppermute(head, axis, [((i + 1) % count, i) for i in range(count)])]
    unnamed x38 -> x2, local copies, waits for them, and re-layouts: 10.5 us -> 0.01 us
    reshape x0 -> x4, local copies, waits for them, and re-layouts: none -> 4.19 us  [the longest x1 1.48 us: local_kernel(): activations.reshape(rows, -1)]
  transfers between devices with their start and end apart: 8 -> 0, of which waited for: 3 -> 0; matrix products, arithmetic and copies ran while one was open for 13% -> 0% of each run, Pallas kernels for 0% -> 0%
where the time goes in v1:
time: 68.5 us; the launch traced here: 68.3 us
  Pallas kernels  62.7 us (92%)
  local copies, waits for them, and re-layouts  4.97 us (7%)
    pallas_call x1, Pallas kernels, local_kernel(): pl.pallas_call(functools.partial(kernel, (n, m, rows, block, depth, heigh...  62.7 us
    reshape x1, local copies, waits for them, and re-layouts, local_kernel(): activations.reshape(rows, -1)  1.48 us

profile of v1, /device:TPU:0, one launch (start us, length us, event | category | flops | bytes accessed | tf_op | source)
XLA Modules:
  0.0 68.3 jit_solution(16593645761666801278)
XLA Ops:
  0.6 0.8 %fusion.wsl = bf16[4,32,128]{2,1,0:T(8,128)(2,1)S(1)} fusion(s32[]{:T(128)S(6)} %select_n.3, bf16[27,128,32]{1,2,0:T(8,128)(2,1)} %param.4), kind=kLoop, calls=%fused_computation.1 | loop fusion | bytes 253956 | tf_op jit(solution)/shard_map/transpose | solution.py:281
  1.4 0.0 copy-start
  1.4 1.5 %reshape.16.act = bf16[32,8192]{1,0:T(8,128)(2,1)S(1)} reshape(bf16[32,16,4,128]{3,2,1,0:T(4,128)(2,1)} %param.3) | data formatting | bytes 1048576 | tf_op jit(solution)/shard_map/reshape | solution.py:309
  2.9 0.0 copy-done
  2.9 0.4 reshape.17.grad
  3.3 62.7 %shard_map.50 = (bf16[32,8192]{1,0:T(8,128)(2,1)S(1)}, bf16[32,8192]{1,0:T(8,128)(2,1)S(1)}) custom-call(bf16[32,8192]{1,0:T(8,128)(2,1)S(1)} %reshape.16.act, bf16[32,8192]{1,0:T(8,128)(2,1)S(1)} %reshape.17.grad, bf16[4,32,128]{2,1,0:T(8,128)(2,1)S(1)} %fusion.wsl), custom_call_target="tpu_custom_call" | custom-call | flops 3623878656 | bytes 2097152 | tf_op jit(solution)/shard_map/pallas_call | solution.py:286
  66.0 1.2 %reshape.18 = bf16[32,16,4,128]{3,2,1,0:T(4,128)(2,1)} reshape(bf16[32,8192]{1,0:T(8,128)(2,1)S(1)} %get-tuple-element.4) | data formatting | bytes 1048576 | tf_op jit(solution)/shard_map/reshape | solution.py:310
  67.1 1.2 %reshape.19 = bf16[32,16,4,128]{3,2,1,0:T(4,128)(2,1)} reshape(bf16[32,8192]{1,0:T(8,128)(2,1)S(1)} %get-tuple-element.5) | data formatting | bytes 1048576 | tf_op jit(solution)/shard_map/reshape | solution.py:310
Async XLA Ops:
  1.4 1.5 %copy-start = (bf16[32,16,4,128]{3,2,1,0:T(4,128)(2,1)S(1)}, bf16[32,16,4,128]{3,2,1,0:T(4,128)(2,1)}, u32[]{:S(2)}) copy-start(bf16[32,16,4,128]{3,2,1,0:T(4,128)(2,1)} %param.5) | copy-start | bytes 1572868

commit v2 on v1

--- a/solution.py
+++ b/solution.py
@@ -78,7 +78,7 @@
     dims, act, grad, wsl, outf, outg,
     xa, xg, gathered, lf, lb, yf, yg,
     w1_send, w1_recv, w2_send, w2_recv, in_send, in_recv, halo_send, halo_recv,
-    out_send, out_recv, own,
+    out_send, out_recv, extra_send, extra_recv, own,
 ):
     n, m, rows, block, depth, height, taps = dims
     chans = m * rows
@@ -143,6 +143,50 @@
             in_send.at[which, r], in_recv.at[which, r], (g, dd),
         )
 
+    def middle(kk):
+        return jnp.logical_or(kk == m // 2 - 1, kk == m // 2)
+
+    def extra_cols(kk):
+        upper = kk == m // 2
+        src = jnp.where(upper, kk * span - plane, (kk + 1) * span)
+        dst = jnp.where(upper, 0, span + plane)
+        return pl.ds(pl.multiple_of(src, 128), plane), pl.ds(pl.multiple_of(dst, 128), plane)
+
+    def extra(which, x, field, r, sending):
+        dd = lax.rem(d + r, m) if sending else lax.rem(d + m - r, m)
+        at = d if sending else dd
+        src, dst = extra_cols(block_of(g, dd) if sending else k)
+        return remote(
+            field.at[:, src], x.at[rows_at(at), dst],
+            extra_send.at[which, r], extra_recv.at[which, r], (g, dd),
+        )
+
+    def goes(r):
+        return middle(block_of(g, lax.rem(d + r, m)))
+
+    def spread_start(which, x, field, r):
+        spread(which, x, field, r, True).start()
+
+        @pl.when(goes(r))
+        def _():
+            extra(which, x, field, r, True).start()
+
+    def spread_sent(which, x, field, r):
+        spread(which, x, field, r, True).wait_send()
+
+        @pl.when(goes(r))
+        def _():
+            extra(which, x, field, r, True).wait_send()
+
+    def spread_landed(which, x, field):
+        for r in others:
+            spread(which, x, field, r, False).wait_recv()
+
+        @pl.when(middle(k))
+        def _():
+            for r in others:
+                extra(which, x, field, r, False).wait_recv()
+
     def halo(which, x, side):
         first, last = pl.ds(plane, plane), pl.ds(span, plane)
         low, high = pl.ds(0, plane), pl.ds(span + plane, plane)
@@ -151,12 +195,38 @@
             x.at[:, src], x.at[:, dst], halo_send.at[which, side], halo_recv.at[which, side], where
         )
 
-    def collect(which, y, out, r, sending):
+    has_prev, has_next = k != m // 2, k != m // 2 - 1
+    sends, lands = (has_prev, has_next), (has_next, has_prev)
+
+    def halo_start(which, x):
+        for side in range(2):
+            @pl.when(sends[side])
+            def _():
+                halo(which, x, side).start()
+
+    def halo_sent(which, x):
+        for side in range(2):
+            @pl.when(sends[side])
+            def _():
+                halo(which, x, side).wait_send()
+
+    def halo_landed(which, x):
+        for side in range(2):
+            @pl.when(lands[side])
+            def _():
+                halo(which, x, side).wait_recv()
+
+    pieces = [(0, plane), ((block - 1) * plane, plane)]
+    if block > 2:
+        pieces.append((plane, (block - 2) * plane))
+
+    def collect(which, y, out, j, r, sending):
         dd = lax.rem(d + r, m) if sending else lax.rem(d + m - r, m)
         at = k if sending else block_of(g, dd)
         return remote(
-            y.at[rows_at(dd if sending else d), :], out.at[:, cols_at(at)],
-            out_send.at[which, r], out_recv.at[which, r], (g, dd),
+            y.at[rows_at(dd if sending else d), pl.ds(*pieces[j])],
+            out.at[:, pl.ds(pl.multiple_of(at * span + pieces[j][0], 128), pieces[j][1])],
+            out_send.at[which, j, r], out_recv.at[which, j, r], (g, dd),
         )
 
     own_copies = [
@@ -165,10 +235,24 @@
         pltpu.make_async_copy(grad.at[:, cols_at(k)], xg.at[rows_at(d), pl.ds(plane, span)], own.at[2]),
     ]
     others, peers = range(1, m), range(1, n)
-    for r in others:
+    even = lax.rem(d, 2) == 0
+    order = [m // 2] + [
+        r
+        for i in range(1, m - m // 2)
+        for r in (jnp.where(even, m // 2 + i, m // 2 - i), jnp.where(even, m // 2 - i, m // 2 + i))
+    ]
+    for r in order:
         w1(r, True).start()
-    for r in others:
-        spread(0, xa, act, r, True).start()
+    for r in order:
+        spread_start(0, xa, act, r)
+    for which, x, field in ((0, xa, act), (1, xg, grad)):
+        @pl.when(middle(k))
+        def _():
+            src, dst = extra_cols(k)
+            c = pltpu.make_async_copy(field.at[:, src], x.at[rows_at(d), dst], own.at[3 + which])
+            c.start()
+            c.wait()
+
     for c in own_copies:
         c.start()
     for c in own_copies:
@@ -181,14 +265,11 @@
         for r in peers:
             w2(r, True).start()
 
-    for r in others:
-        spread(0, xa, act, r, True).wait_send()
-    for r in others:
-        spread(1, xg, grad, r, True).start()
-    for r in others:
-        spread(0, xa, act, r, False).wait_recv()
-    for side in range(2):
-        halo(0, xa, side).start()
+    for r in order:
+        spread_sent(0, xa, act, r)
+        spread_start(1, xg, grad, r)
+    spread_landed(0, xa, act)
+    halo_start(0, xa)
 
     for r in peers:
         @pl.when(lax.rem(g + n - r, n) * per < taps)
@@ -234,34 +315,34 @@
     def finish(which, x, l, y, out):
         for s in range(2, block, 2):
             pair_sum(x, l, y, (s, s + 1))
-        for side in range(2):
-            halo(which, x, side).wait_recv()
+        if block > 2:
+            for r in order:
+                collect(which, y, out, 2, r, True).start()
+        halo_landed(which, x)
         pair_sum(x, l, y, (1, block))
-        for r in others:
-            collect(which, y, out, r, True).start()
+        for r in order:
+            for j in range(2):
+                collect(which, y, out, j, r, True).start()
         copy = pltpu.make_async_copy(y.at[rows_at(d), :], out.at[:, cols_at(k)], own.at[3 + which])
         copy.start()
         return copy
 
     first_own = finish(0, xa, lf, yf, outf)
-    for r in others:
-        spread(1, xg, grad, r, False).wait_recv()
-    for side in range(2):
-        halo(1, xg, side).start()
+    spread_landed(1, xg, grad)
+    halo_start(1, xg)
     second_own = finish(1, xg, lb, yg, outg)
 
     first_own.wait()
     second_own.wait()
     for r in others:
-        collect(0, yf, outf, r, False).wait_recv()
-        collect(1, yg, outg, r, False).wait_recv()
         w1(r, True).wait_send()
-        spread(1, xg, grad, r, True).wait_send()
-        collect(0, yf, outf, r, True).wait_send()
-        collect(1, yg, outg, r, True).wait_send()
-    for which, x in ((0, xa), (1, xg)):
-        for side in range(2):
-            halo(which, x, side).wait_send()
+        spread_sent(1, xg, grad, r)
+        for which, y, out in ((0, yf, outf), (1, yg, outg)):
+            for j in range(len(pieces)):
+                collect(which, y, out, j, r, False).wait_recv()
+                collect(which, y, out, j, r, True).wait_send()
+    halo_sent(0, xa)
+    halo_sent(1, xg)
 
     @pl.when(g * per < taps)
     def _():
@@ -298,10 +379,10 @@
             pltpu.VMEM((chans, block * plane), jnp.bfloat16),
             sem((m,)), sem((m,)), sem((n,)), sem((n,)),
             sem((2, m)), sem((2, m)), sem((2, 2)), sem((2, 2)),
-            sem((2, m)), sem((2, m)), sem((5,)),
+            sem((2, 3, m)), sem((2, 3, m)), sem((2, m)), sem((2, m)), sem((5,)),
         ],
         compiler_params=pltpu.CompilerParams(
-            collective_id=0, has_side_effects=True, vmem_limit_bytes=40 * 2**20
+            collective_id=0, has_side_effects=True, vmem_limit_bytes=20 * 2**20
         ),
         cost_estimate=pl.CostEstimate(
             flops=flops, bytes_accessed=8 * rows * planes * plane, transcendentals=0
@@ -313,7 +394,7 @@
 def local(activations, conv_weight, out_grad):
     n, m = lax.axis_size("gx"), lax.axis_size("ch")
     rows, planes, _, height = activations.shape
-    fits = rows % 16 == 0 and planes % (2 * m) == 0 and height % 128 == 0 and n % 2 == 0
+    fits = rows % 16 == 0 and planes % (2 * m) == 0 and height % 128 == 0 and n % 2 == 0 and m % 2 == 0
     plan = local_kernel if fits else local_plain
     return plan(activations, conv_weight, out_grad)
 

time: 68.5 us -> 65 us (0.949)
  Pallas kernels: 62.7 us -> 59.2 us
    pallas_call x1, Pallas kernels: 62.7 us -> 59.2 us  [local_kernel(): pl.pallas_call(functools.partial(kernel, (n, m, rows, block, depth, heigh...]
where the time goes in v2:
time: 65 us; the launch traced here: 64.8 us
  Pallas kernels  59.2 us (91%)
  local copies, waits for them, and re-layouts  4.97 us (8%)
  between operations  0.67 us (1%)
    pallas_call x1, Pallas kernels, local_kernel(): pl.pallas_call(functools.partial(kernel, (n, m, rows, block, depth, heigh...  59.2 us
    reshape x1, local copies, waits for them, and re-layouts, local_kernel(): activations.reshape(rows, -1)  1.48 us

profile of v2, /device:TPU:0, one launch (start us, length us, event | category | flops | bytes accessed | tf_op | source)
XLA Modules:
  0.0 64.8 jit_solution(12155694553395634262)
XLA Ops:
  0.6 0.8 %fusion.wsl = bf16[4,32,128]{2,1,0:T(8,128)(2,1)S(1)} fusion(s32[]{:T(128)S(6)} %select_n.3, bf16[27,128,32]{1,2,0:T(8,128)(2,1)} %param.4), kind=kLoop, calls=%fused_computation.1 | loop fusion | bytes 253956 | tf_op jit(solution)/shard_map/transpose | solution.py:362
  1.4 0.0 copy-start
  1.4 1.5 %reshape.16.act = bf16[32,8192]{1,0:T(8,128)(2,1)S(1)} reshape(bf16[32,16,4,128]{3,2,1,0:T(4,128)(2,1)} %param.3) | data formatting | bytes 1048576 | tf_op jit(solution)/shard_map/reshape | solution.py:390
  2.9 0.0 copy-done
  2.9 0.4 reshape.17.grad
  3.3 59.2 %shard_map.50 = (bf16[32,8192]{1,0:T(8,128)(2,1)S(1)}, bf16[32,8192]{1,0:T(8,128)(2,1)S(1)}) custom-call(bf16[32,8192]{1,0:T(8,128)(2,1)S(1)} %reshape.16.act, bf16[32,8192]{1,0:T(8,128)(2,1)S(1)} %reshape.17.grad, bf16[4,32,128]{2,1,0:T(8,128)(2,1)S(1)} %fusion.wsl), custom_call_target="tpu_custom_call" | custom-call | flops 3623878656 | bytes 2097152 | tf_op jit(solution)/shard_map/pallas_call | solution.py:367
  62.5 1.2 %reshape.18 = bf16[32,16,4,128]{3,2,1,0:T(4,128)(2,1)} reshape(bf16[32,8192]{1,0:T(8,128)(2,1)S(1)} %get-tuple-element.4) | data formatting | bytes 1048576 | tf_op jit(solution)/shard_map/reshape | solution.py:391
  63.7 1.2 %reshape.19 = bf16[32,16,4,128]{3,2,1,0:T(4,128)(2,1)} reshape(bf16[32,8192]{1,0:T(8,128)(2,1)S(1)} %get-tuple-element.5) | data formatting | bytes 1048576 | tf_op jit(solution)/shard_map/reshape | solution.py:391
Async XLA Ops:
  1.4 1.5 %copy-start = (bf16[32,16,4,128]{3,2,1,0:T(4,128)(2,1)S(1)}, bf16[32,16,4,128]{3,2,1,0:T(4,128)(2,1)}, u32[]{:S(2)}) copy-start(bf16[32,16,4,128]{3,2,1,0:T(4,128)(2,1)} %param.5) | copy-start | bytes 1572868

commit v3 on v2

--- a/solution.py
+++ b/solution.py
@@ -75,14 +75,15 @@
 
 
 def kernel(
-    dims, act, grad, wsl, outf, outg,
+    dims, act_hbm, grad_hbm, weight_hbm, out_features, out_gradient,
+    act_raw, grad_raw, act, grad, wsl, outf, outg,
     xa, xg, gathered, lf, lb, yf, yg,
     w1_send, w1_recv, w2_send, w2_recv, in_send, in_recv, halo_send, halo_recv,
-    out_send, out_recv, extra_send, extra_recv, own,
+    out_send, out_recv, extra_send, extra_recv, own, w_in,
 ):
     n, m, rows, block, depth, height, taps = dims
     chans = m * rows
-    per = wsl.shape[0]
+    per = -(-taps // n)
     plane = depth * height
     span = block * plane
     g = lax.axis_index("gx")
@@ -107,12 +108,36 @@
 
     def cols_at(kk):
         return pl.ds(pl.multiple_of(kk * span, 128), span)
+
+    loads = [
+        pltpu.make_async_copy(act_hbm, act_raw, own.at[5]),
+        pltpu.make_async_copy(grad_hbm, grad_raw, own.at[6]),
+    ]
+    taps_in = [
+        pltpu.make_async_copy(
+            weight_hbm.at[jnp.minimum(g * per + i, taps - 1)], wsl.at[i], w_in.at[i]
+        )
+        for i in range(per)
+    ]
+    loads[0].start()
+    for c in taps_in:
+        c.start()
+    loads[1].start()
 
     barrier = pltpu.get_barrier_semaphore()
     for r in range(1, m):
         pl.semaphore_signal(barrier, inc=1, device_id=(g, lax.rem(d + r, m)), device_id_type=MESH)
     for r in range(1, n):
         pl.semaphore_signal(barrier, inc=1, device_id=(lax.rem(g + r, n), d), device_id_type=MESH)
+
+    def flatten(raw, field):
+        for p in range(block * m):
+            field[:, pl.ds(p * plane, plane)] = raw[:, p].reshape(rows, plane)
+
+    for c in taps_in:
+        c.wait()
+    loads[0].wait()
+    flatten(act_raw, act)
     pl.semaphore_wait(barrier, m - 1 + n - 1)
 
     def remote(src, dst, send, recv, where):
@@ -245,6 +270,8 @@
         w1(r, True).start()
     for r in order:
         spread_start(0, xa, act, r)
+    loads[1].wait()
+    flatten(grad_raw, grad)
     for which, x, field in ((0, xa, act), (1, xg, grad)):
         @pl.when(middle(k))
         def _():
@@ -276,12 +303,15 @@
         def _():
             w2(r, False).wait_recv()
 
-    for a in range(3):
-        for b in range(3):
-            for c in range(3):
-                at = pl.ds((3 * c + a) * chans, chans)
-                lf[pl.ds(b * chans, chans), at] = gathered[9 * a + 3 * b + c]
-                lb[pl.ds(b * chans, chans), at] = gathered[9 * (2 - a) + 3 * (2 - b) + 2 - c].T
+    def filters(l, backward):
+        for a in range(3):
+            for b in range(3):
+                for c in range(3):
+                    tap = 9 * a + 3 * b + c
+                    block_at = gathered[26 - tap].T if backward else gathered[tap]
+                    l[pl.ds(b * chans, chans), pl.ds((3 * c + a) * chans, chans)] = block_at
+
+    filters(lf, False)
 
     lane = lax.broadcasted_iota(jnp.int32, (chans, height), 1)
 
@@ -328,21 +358,36 @@
         return copy
 
     first_own = finish(0, xa, lf, yf, outf)
+    filters(lb, True)
     spread_landed(1, xg, grad)
     halo_start(1, xg)
     second_own = finish(1, xg, lb, yg, outg)
 
-    first_own.wait()
-    second_own.wait()
+    def unflatten(which, y, out, staged, result, own_copy):
+        own_copy.wait()
+        for r in others:
+            for j in range(len(pieces)):
+                collect(which, y, out, j, r, False).wait_recv()
+        for p in range(block * m):
+            staged[:, p] = out[:, pl.ds(p * plane, plane)].reshape(rows, depth, height)
+        copy = pltpu.make_async_copy(staged, result, own.at[5 + which])
+        copy.start()
+        return copy
+
+    stores = [
+        unflatten(0, yf, outf, act_raw, out_features, first_own),
+        unflatten(1, yg, outg, grad_raw, out_gradient, second_own),
+    ]
     for r in others:
         w1(r, True).wait_send()
         spread_sent(1, xg, grad, r)
         for which, y, out in ((0, yf, outf), (1, yg, outg)):
             for j in range(len(pieces)):
-                collect(which, y, out, j, r, False).wait_recv()
                 collect(which, y, out, j, r, True).wait_send()
     halo_sent(0, xa)
     halo_sent(1, xg)
+    for c in stores:
+        c.wait()
 
     @pl.when(g * per < taps)
     def _():
@@ -357,19 +402,24 @@
     block = planes // m
     plane = depth * height
     per = -(-taps // n)
-    padded = jnp.pad(conv_weight, ((0, per * n - taps), (0, 0), (0, 0)))
-    wsl = lax.dynamic_slice_in_dim(padded, lax.axis_index("gx") * per, per, axis=0)
-    wsl = jnp.swapaxes(wsl, 1, 2)
-    vmem = pl.BlockSpec(memory_space=pltpu.VMEM)
-    flat = jax.ShapeDtypeStruct((rows, planes * plane), jnp.bfloat16)
+    whole = jax.ShapeDtypeStruct(activations.shape, jnp.bfloat16)
+    flat = pltpu.VMEM((rows, planes * plane), jnp.bfloat16)
+    raw = pltpu.VMEM(activations.shape, jnp.bfloat16)
     sem = pltpu.SemaphoreType.DMA
     flops = 2 * 2 * taps * chans * chans * block * plane
     features, gradient = pl.pallas_call(
         functools.partial(kernel, (n, m, rows, block, depth, height, taps)),
-        out_shape=(flat, flat),
-        in_specs=[vmem] * 3,
-        out_specs=(vmem, vmem),
+        out_shape=(whole, whole),
+        in_specs=[pl.BlockSpec(memory_space=pl.ANY)] * 3,
+        out_specs=(pl.BlockSpec(memory_space=pl.ANY),) * 2,
         scratch_shapes=[
+            raw,
+            raw,
+            flat,
+            flat,
+            pltpu.VMEM((per, rows, chans), jnp.bfloat16),
+            flat,
+            flat,
             pltpu.VMEM((chans, (block + 2) * plane), jnp.bfloat16),
             pltpu.VMEM((chans, (block + 2) * plane), jnp.bfloat16),
             pltpu.VMEM((per * n, chans, chans), jnp.bfloat16),
@@ -379,16 +429,16 @@
             pltpu.VMEM((chans, block * plane), jnp.bfloat16),
             sem((m,)), sem((m,)), sem((n,)), sem((n,)),
             sem((2, m)), sem((2, m)), sem((2, 2)), sem((2, 2)),
-            sem((2, 3, m)), sem((2, 3, m)), sem((2, m)), sem((2, m)), sem((5,)),
+            sem((2, 3, m)), sem((2, 3, m)), sem((2, m)), sem((2, m)), sem((7,)), sem((per,)),
         ],
         compiler_params=pltpu.CompilerParams(
-            collective_id=0, has_side_effects=True, vmem_limit_bytes=20 * 2**20
+            collective_id=0, has_side_effects=True, vmem_limit_bytes=60 * 2**20
         ),
         cost_estimate=pl.CostEstimate(
             flops=flops, bytes_accessed=8 * rows * planes * plane, transcendentals=0
         ),
-    )(activations.reshape(rows, -1), out_grad.reshape(rows, -1), wsl)
-    return features.reshape(activations.shape), gradient.reshape(out_grad.shape)
+    )(activations, out_grad, jnp.swapaxes(conv_weight, 1, 2))
+    return features, gradient
 
 
 def local(activations, conv_weight, out_grad):

time: 65 us -> 64.3 us (0.989)
  local copies, waits for them, and re-layouts: 4.97 us -> 2.91 us
  Pallas kernels: 59.2 us -> 60.6 us
    reshape x4 -> x0, local copies, waits for them, and re-layouts: 4.19 us -> none  [the longest x1 1.48 us: local_kernel(): activations.reshape(rows, -1)]
    unnamed x2 -> x4, local copies, waits for them, and re-layouts: 0.01 us -> 2.91 us
    pallas_call x1, Pallas kernels: 59.2 us -> 60.6 us  [local_kernel(): pl.pallas_call(functools.partial(kernel, (n, m, rows, block, depth, heigh...]
    transpose x1 -> x0, local copies, waits for them, and re-layouts: 0.78 us -> none  [local_kernel(): wsl = jnp.swapaxes(wsl, 1, 2)]
where the time goes in v3:
time: 64.3 us; the launch traced here: 64.1 us
  Pallas kernels  60.6 us (94%)
  local copies, waits for them, and re-layouts  2.91 us (5%)
  between operations  0.65 us (1%)
    pallas_call x1, Pallas kernels, local_kernel(): pl.pallas_call(functools.partial(kernel, (n, m, rows, block, depth, heigh...  60.6 us
    unnamed x4, local copies, waits for them, and re-layouts  2.91 us

profile of v3, /device:TPU:0, one launch (start us, length us, event | category | flops | bytes accessed | tf_op | source)
XLA Modules:
  0.0 64.1 jit_solution(5770683606727851528)
XLA Ops:
  0.6 60.6 %shard_map.50 = (bf16[32,16,4,128]{3,2,1,0:T(4,128)(2,1)}, bf16[32,16,4,128]{3,2,1,0:T(4,128)(2,1)}) custom-call(bf16[32,16,4,128]{3,2,1,0:T(4,128)(2,1)} %act_hbm.1, bf16[32,16,4,128]{3,2,1,0:T(4,128)(2,1)} %grad_hbm.1, bf16[27,32,128]{2,1,0:T(8,128)(2,1)} %bitcast.1), custom_call_target="tpu_custom_call" | custom-call | flops 3623878656 | bytes 2097152 | tf_op jit(solution)/shard_map/pallas_call | solution.py:410
  61.2 0.0 copy-start
  61.2 2.1 %copy.7 = bf16[32,16,4,128]{3,2,1,0:T(4,128)(2,1)} copy(bf16[32,16,4,128]{3,2,1,0:T(4,128)(2,1)} %get-tuple-element.4) | data formatting | bytes 1048576
  63.3 0.0 copy-done
  63.3 0.8 %copy.8 = bf16[32,16,4,128]{3,2,1,0:T(4,128)(2,1)} copy(bf16[32,16,4,128]{3,2,1,0:T(4,128)(2,1)S(1)} %copy-done) | data formatting | bytes 1048576
Async XLA Ops:
  61.2 2.1 %copy-start = (bf16[32,16,4,128]{3,2,1,0:T(4,128)(2,1)S(1)}, bf16[32,16,4,128]{3,2,1,0:T(4,128)(2,1)}, u32[]{:S(2)}) copy-start(bf16[32,16,4,128]{3,2,1,0:T(4,128)(2,1)} %get-tuple-element.5) | copy-start | bytes 1572868

commit v4 on v3

--- a/solution.py
+++ b/solution.py
@@ -75,11 +75,11 @@
 
 
 def kernel(
-    dims, act_hbm, grad_hbm, weight_hbm, out_features, out_gradient,
-    act_raw, grad_raw, act, grad, wsl, outf, outg,
+    dims, act_raw, grad_raw, weight, out_features, out_gradient,
+    act, grad, wsl, outf, outg,
     xa, xg, gathered, lf, lb, yf, yg,
     w1_send, w1_recv, w2_send, w2_recv, in_send, in_recv, halo_send, halo_recv,
-    out_send, out_recv, extra_send, extra_recv, own, w_in,
+    out_send, out_recv, extra_send, extra_recv, own,
 ):
     n, m, rows, block, depth, height, taps = dims
     chans = m * rows
@@ -109,21 +109,6 @@
     def cols_at(kk):
         return pl.ds(pl.multiple_of(kk * span, 128), span)
 
-    loads = [
-        pltpu.make_async_copy(act_hbm, act_raw, own.at[5]),
-        pltpu.make_async_copy(grad_hbm, grad_raw, own.at[6]),
-    ]
-    taps_in = [
-        pltpu.make_async_copy(
-            weight_hbm.at[jnp.minimum(g * per + i, taps - 1)], wsl.at[i], w_in.at[i]
-        )
-        for i in range(per)
-    ]
-    loads[0].start()
-    for c in taps_in:
-        c.start()
-    loads[1].start()
-
     barrier = pltpu.get_barrier_semaphore()
     for r in range(1, m):
         pl.semaphore_signal(barrier, inc=1, device_id=(g, lax.rem(d + r, m)), device_id_type=MESH)
@@ -134,9 +119,8 @@
         for p in range(block * m):
             field[:, pl.ds(p * plane, plane)] = raw[:, p].reshape(rows, plane)
 
-    for c in taps_in:
-        c.wait()
-    loads[0].wait()
+    for i in range(per):
+        wsl[i] = weight[jnp.minimum(g * per + i, taps - 1)]
     flatten(act_raw, act)
     pl.semaphore_wait(barrier, m - 1 + n - 1)
 
@@ -270,7 +254,6 @@
         w1(r, True).start()
     for r in order:
         spread_start(0, xa, act, r)
-    loads[1].wait()
     flatten(grad_raw, grad)
     for which, x, field in ((0, xa, act), (1, xg, grad)):
         @pl.when(middle(k))
@@ -363,21 +346,16 @@
     halo_start(1, xg)
     second_own = finish(1, xg, lb, yg, outg)
 
-    def unflatten(which, y, out, staged, result, own_copy):
+    def unflatten(which, y, out, result, own_copy):
         own_copy.wait()
         for r in others:
             for j in range(len(pieces)):
                 collect(which, y, out, j, r, False).wait_recv()
         for p in range(block * m):
-            staged[:, p] = out[:, pl.ds(p * plane, plane)].reshape(rows, depth, height)
-        copy = pltpu.make_async_copy(staged, result, own.at[5 + which])
-        copy.start()
-        return copy
-
-    stores = [
-        unflatten(0, yf, outf, act_raw, out_features, first_own),
-        unflatten(1, yg, outg, grad_raw, out_gradient, second_own),
-    ]
+            result[:, p] = out[:, pl.ds(p * plane, plane)].reshape(rows, depth, height)
+
+    unflatten(0, yf, outf, out_features, first_own)
+    unflatten(1, yg, outg, out_gradient, second_own)
     for r in others:
         w1(r, True).wait_send()
         spread_sent(1, xg, grad, r)
@@ -386,13 +364,22 @@
                 collect(which, y, out, j, r, True).wait_send()
     halo_sent(0, xa)
     halo_sent(1, xg)
-    for c in stores:
-        c.wait()
 
     @pl.when(g * per < taps)
     def _():
         for r in peers:
             w2(r, True).wait_send()
+
+
+def store(features, gradient, out_features, out_gradient, sems):
+    copies = [
+        pltpu.make_async_copy(features, out_features, sems.at[0]),
+        pltpu.make_async_copy(gradient, out_gradient, sems.at[1]),
+    ]
+    for c in copies:
+        c.start()
+    for c in copies:
+        c.wait()
 
 
 def local_kernel(activations, conv_weight, out_grad):
@@ -404,17 +391,16 @@
     per = -(-taps // n)
     whole = jax.ShapeDtypeStruct(activations.shape, jnp.bfloat16)
     flat = pltpu.VMEM((rows, planes * plane), jnp.bfloat16)
-    raw = pltpu.VMEM(activations.shape, jnp.bfloat16)
+    vmem = pl.BlockSpec(memory_space=pltpu.VMEM)
+    hbm = pl.BlockSpec(memory_space=pl.ANY)
     sem = pltpu.SemaphoreType.DMA
     flops = 2 * 2 * taps * chans * chans * block * plane
     features, gradient = pl.pallas_call(
         functools.partial(kernel, (n, m, rows, block, depth, height, taps)),
         out_shape=(whole, whole),
-        in_specs=[pl.BlockSpec(memory_space=pl.ANY)] * 3,
-        out_specs=(pl.BlockSpec(memory_space=pl.ANY),) * 2,
+        in_specs=[vmem] * 3,
+        out_specs=(vmem, vmem),
         scratch_shapes=[
-            raw,
-            raw,
             flat,
             flat,
             pltpu.VMEM((per, rows, chans), jnp.bfloat16),
@@ -429,16 +415,22 @@
             pltpu.VMEM((chans, block * plane), jnp.bfloat16),
             sem((m,)), sem((m,)), sem((n,)), sem((n,)),
             sem((2, m)), sem((2, m)), sem((2, 2)), sem((2, 2)),
-            sem((2, 3, m)), sem((2, 3, m)), sem((2, m)), sem((2, m)), sem((7,)), sem((per,)),
+            sem((2, 3, m)), sem((2, 3, m)), sem((2, m)), sem((2, m)), sem((5,)),
         ],
         compiler_params=pltpu.CompilerParams(
-            collective_id=0, has_side_effects=True, vmem_limit_bytes=60 * 2**20
+            collective_id=0, has_side_effects=True, vmem_limit_bytes=28 * 2**20
         ),
         cost_estimate=pl.CostEstimate(
             flops=flops, bytes_accessed=8 * rows * planes * plane, transcendentals=0
         ),
     )(activations, out_grad, jnp.swapaxes(conv_weight, 1, 2))
-    return features, gradient
+    return pl.pallas_call(
+        store,
+        out_shape=(whole, whole),
+        in_specs=[vmem] * 2,
+        out_specs=(hbm, hbm),
+        scratch_shapes=[sem((2,))],
+    )(features, gradient)
 
 
 def local(activations, conv_weight, out_grad):

time: 64.3 us -> 67.2 us (1.045)
  local copies, waits for them, and re-layouts: 2.91 us -> 4.58 us
  Pallas kernels: 60.6 us -> 61.7 us
    pallas_call x0 -> x1, Pallas kernels: none -> 2.18 us  [local_kernel(): pl.pallas_call(store, out_shape=(whole, whole), in_specs=[vmem] * 2, out_...]
    unnamed x4 -> x10, local copies, waits for them, and re-layouts: 2.91 us -> 4.58 us
    pallas_call x1, Pallas kernels: 60.6 us -> 59.6 us  [local_kernel(): pl.pallas_call(functools.partial(kernel, (n, m, rows, block, depth, heigh...]
where the time goes in v4:
time: 67.2 us; the launch traced here: 67 us
  Pallas kernels  61.7 us (92%)
  local copies, waits for them, and re-layouts  4.58 us (7%)
    pallas_call x1, Pallas kernels, local_kernel(): pl.pallas_call(functools.partial(kernel, (n, m, rows, block, depth, heigh...  59.6 us
    unnamed x10, local copies, waits for them, and re-layouts  4.58 us
    pallas_call x1, Pallas kernels, local_kernel(): pl.pallas_call(store, out_shape=(whole, whole), in_specs=[vmem] * 2, out_...  2.18 us

profile of v4, /device:TPU:0, one launch (start us, length us, event | category | flops | bytes accessed | tf_op | source)
XLA Modules:
  0.0 67.0 jit_solution(2993423277438868902)
XLA Ops:
  0.6 0.0 copy-start.2
  0.6 1.0 %copy-done.2 = bf16[32,16,4,128]{3,2,1,0:T(4,128)(2,1)S(1)} copy-done((bf16[32,16,4,128]{3,2,1,0:T(4,128)(2,1)S(1)}, bf16[32,16,4,128]{3,2,1,0:T(4,128)(2,1)}, u32[]{:S(2)}) %copy-start.2) | copy-done | bytes 524312
  1.7 0.0 copy-start.3
  1.7 1.0 %copy-done.3 = bf16[32,16,4,128]{3,2,1,0:T(4,128)(2,1)S(1)} copy-done((bf16[32,16,4,128]{3,2,1,0:T(4,128)(2,1)S(1)}, bf16[32,16,4,128]{3,2,1,0:T(4,128)(2,1)}, u32[]{:S(2)}) %copy-start.3) | copy-done | bytes 524312
  2.7 0.0 copy-start.4
  2.7 0.9 %copy-done.4 = bf16[27,128,32]{1,2,0:T(8,128)(2,1)S(1)} copy-done((bf16[27,128,32]{1,2,0:T(8,128)(2,1)S(1)}, bf16[27,128,32]{1,2,0:T(8,128)(2,1)}, u32[]{:S(2)}) %copy-start.4) | copy-done | bytes 221208
  3.7 59.6 %shard_map.50 = (bf16[32,16,4,128]{3,2,1,0:T(4,128)(2,1)S(1)}, bf16[32,16,4,128]{3,2,1,0:T(4,128)(2,1)S(1)}) custom-call(bf16[32,16,4,128]{3,2,1,0:T(4,128)(2,1)S(1)} %copy-done.2, bf16[32,16,4,128]{3,2,1,0:T(4,128)(2,1)S(1)} %copy-done.3, bf16[27,32,128]{2,1,0:T(8,128)(2,1)S(1)} %bitcast.1), custom_call_target="tpu_custom_call" | custom-call | flops 3623878656 | bytes 2097152 | tf_op jit(solution)/shard_map/pallas_call | solution.py:398
  63.2 0.0 copy-start
  63.2 0.8 %copy-done = bf16[32,16,4,128]{3,2,1,0:T(4,128)(2,1)} copy-done((bf16[32,16,4,128]{3,2,1,0:T(4,128)(2,1)}, bf16[32,16,4,128]{3,2,1,0:T(4,128)(2,1)S(1)}, u32[]{:S(2)}) %copy-start) | copy-done | bytes 524312
  64.0 0.0 copy-start.1
  64.0 0.8 %copy-done.1 = bf16[32,16,4,128]{3,2,1,0:T(4,128)(2,1)} copy-done((bf16[32,16,4,128]{3,2,1,0:T(4,128)(2,1)}, bf16[32,16,4,128]{3,2,1,0:T(4,128)(2,1)S(1)}, u32[]{:S(2)}) %copy-start.1) | copy-done | bytes 524312
  64.8 2.2 %shard_map.51 = (bf16[32,16,4,128]{3,2,1,0:T(4,128)(2,1)}, bf16[32,16,4,128]{3,2,1,0:T(4,128)(2,1)}) custom-call(bf16[32,16,4,128]{3,2,1,0:T(4,128)(2,1)} %copy-done, bf16[32,16,4,128]{3,2,1,0:T(4,128)(2,1)} %copy-done.1), custom_call_target="tpu_custom_call" | custom-call | tf_op jit(solution)/shard_map/pallas_call | solution.py:427
Async XLA Ops:
  0.6 1.0 %copy-start.2 = (bf16[32,16,4,128]{3,2,1,0:T(4,128)(2,1)S(1)}, bf16[32,16,4,128]{3,2,1,0:T(4,128)(2,1)}, u32[]{:S(2)}) copy-start(bf16[32,16,4,128]{3,2,1,0:T(4,128)(2,1)} %act_raw.1) | copy-start | bytes 1572868
  1.7 1.0 %copy-start.3 = (bf16[32,16,4,128]{3,2,1,0:T(4,128)(2,1)S(1)}, bf16[32,16,4,128]{3,2,1,0:T(4,128)(2,1)}, u32[]{:S(2)}) copy-start(bf16[32,16,4,128]{3,2,1,0:T(4,128)(2,1)} %grad_raw.1) | copy-start | bytes 1572868
  2.7 0.9 %copy-start.4 = (bf16[27,128,32]{1,2,0:T(8,128)(2,1)S(1)}, bf16[27,128,32]{1,2,0:T(8,128)(2,1)}, u32[]{:S(2)}) copy-start(bf16[27,128,32]{1,2,0:T(8,128)(2,1)} %param.4) | copy-start | bytes 663556
  63.2 0.8 %copy-start = (bf16[32,16,4,128]{3,2,1,0:T(4,128)(2,1)}, bf16[32,16,4,128]{3,2,1,0:T(4,128)(2,1)S(1)}, u32[]{:S(2)}) copy-start(bf16[32,16,4,128]{3,2,1,0:T(4,128)(2,1)S(1)} %get-tuple-element.4.features) | copy-start | bytes 1572868
  64.0 0.8 %copy-start.1 = (bf16[32,16,4,128]{3,2,1,0:T(4,128)(2,1)}, bf16[32,16,4,128]{3,2,1,0:T(4,128)(2,1)S(1)}, u32[]{:S(2)}) copy-start(bf16[32,16,4,128]{3,2,1,0:T(4,128)(2,1)S(1)} %get-tuple-element.5.gradient) | copy-start | bytes 1572868

commit v5 on v3

--- a/solution.py
+++ b/solution.py
@@ -79,7 +79,7 @@
     act_raw, grad_raw, act, grad, wsl, outf, outg,
     xa, xg, gathered, lf, lb, yf, yg,
     w1_send, w1_recv, w2_send, w2_recv, in_send, in_recv, halo_send, halo_recv,
-    out_send, out_recv, extra_send, extra_recv, own, w_in,
+    out_send, out_recv, extra_send, extra_recv, own, w_in, loaded,
 ):
     n, m, rows, block, depth, height, taps = dims
     chans = m * rows
@@ -109,9 +109,15 @@
     def cols_at(kk):
         return pl.ds(pl.multiple_of(kk * span, 128), span)
 
+    cut = rows // 8
     loads = [
-        pltpu.make_async_copy(act_hbm, act_raw, own.at[5]),
-        pltpu.make_async_copy(grad_hbm, grad_raw, own.at[6]),
+        [
+            pltpu.make_async_copy(
+                src.at[pl.ds(i * cut, cut)], dst.at[pl.ds(i * cut, cut)], loaded.at[which, i]
+            )
+            for i in range(8)
+        ]
+        for which, (src, dst) in enumerate(((act_hbm, act_raw), (grad_hbm, grad_raw)))
     ]
     taps_in = [
         pltpu.make_async_copy(
@@ -119,10 +125,12 @@
         )
         for i in range(per)
     ]
-    loads[0].start()
+    for c in loads[0]:
+        c.start()
     for c in taps_in:
         c.start()
-    loads[1].start()
+    for c in loads[1]:
+        c.start()
 
     barrier = pltpu.get_barrier_semaphore()
     for r in range(1, m):
@@ -136,7 +144,8 @@
 
     for c in taps_in:
         c.wait()
-    loads[0].wait()
+    for c in loads[0]:
+        c.wait()
     flatten(act_raw, act)
     pl.semaphore_wait(barrier, m - 1 + n - 1)
 
@@ -270,7 +279,8 @@
         w1(r, True).start()
     for r in order:
         spread_start(0, xa, act, r)
-    loads[1].wait()
+    for c in loads[1]:
+        c.wait()
     flatten(grad_raw, grad)
     for which, x, field in ((0, xa, act), (1, xg, grad)):
         @pl.when(middle(k))
@@ -370,14 +380,18 @@
                 collect(which, y, out, j, r, False).wait_recv()
         for p in range(block * m):
             staged[:, p] = out[:, pl.ds(p * plane, plane)].reshape(rows, depth, height)
-        copy = pltpu.make_async_copy(staged, result, own.at[5 + which])
-        copy.start()
-        return copy
-
-    stores = [
-        unflatten(0, yf, outf, act_raw, out_features, first_own),
-        unflatten(1, yg, outg, grad_raw, out_gradient, second_own),
-    ]
+        copies = [
+            pltpu.make_async_copy(
+                staged.at[pl.ds(i * cut, cut)], result.at[pl.ds(i * cut, cut)], loaded.at[which, i]
+            )
+            for i in range(8)
+        ]
+        for c in copies:
+            c.start()
+        return copies
+
+    stores = unflatten(0, yf, outf, act_raw, out_features, first_own)
+    stores += unflatten(1, yg, outg, grad_raw, out_gradient, second_own)
     for r in others:
         w1(r, True).wait_send()
         spread_sent(1, xg, grad, r)
@@ -393,6 +407,20 @@
     def _():
         for r in peers:
             w2(r, True).wait_send()
+
+
+def store(cut, features, gradient, out_features, out_gradient, sems):
+    copies = [
+        pltpu.make_async_copy(
+            src.at[pl.ds(i * cut, cut)], dst.at[pl.ds(i * cut, cut)], sems.at[which, i]
+        )
+        for i in range(8)
+        for which, (src, dst) in enumerate(((features, out_features), (gradient, out_gradient)))
+    ]
+    for c in copies:
+        c.start()
+    for c in copies:
+        c.wait()
 
 
 def local_kernel(activations, conv_weight, out_grad):
@@ -429,7 +457,7 @@
             pltpu.VMEM((chans, block * plane), jnp.bfloat16),
             sem((m,)), sem((m,)), sem((n,)), sem((n,)),
             sem((2, m)), sem((2, m)), sem((2, 2)), sem((2, 2)),
-            sem((2, 3, m)), sem((2, 3, m)), sem((2, m)), sem((2, m)), sem((7,)), sem((per,)),
+            sem((2, 3, m)), sem((2, 3, m)), sem((2, m)), sem((2, m)), sem((5,)), sem((per,)), sem((2, 8)),
         ],
         compiler_params=pltpu.CompilerParams(
             collective_id=0, has_side_effects=True, vmem_limit_bytes=60 * 2**20
@@ -438,7 +466,15 @@
             flops=flops, bytes_accessed=8 * rows * planes * plane, transcendentals=0
         ),
     )(activations, out_grad, jnp.swapaxes(conv_weight, 1, 2))
-    return features, gradient
+    hbm = pl.BlockSpec(memory_space=pl.ANY)
+    return pl.pallas_call(
+        functools.partial(store, rows // 8),
+        out_shape=(whole, whole),
+        in_specs=[hbm] * 2,
+        out_specs=(hbm, hbm),
+        scratch_shapes=[sem((2, 8))],
+        compiler_params=pltpu.CompilerParams(vmem_limit_bytes=60 * 2**20),
+    )(features, gradient)
 
 
 def local(activations, conv_weight, out_grad):

time: 64.3 us -> 94.6 us (1.47)
  Pallas kernels: 60.6 us -> 93.8 us
  local copies, waits for them, and re-layouts: 2.91 us -> 0 us
    pallas_call x0 -> x1, Pallas kernels: none -> 33 us  [local_kernel(): pl.pallas_call(functools.partial(store, rows // 8), out_shape=(whole, who...]
    unnamed x4 -> x0, local copies, waits for them, and re-layouts: 2.91 us -> none
where the time goes in v5:
time: 94.6 us; the launch traced here: 94.4 us
  Pallas kernels  93.8 us (99%)
    pallas_call x1, Pallas kernels, local_kernel(): pl.pallas_call(functools.partial(kernel, (n, m, rows, block, depth, heigh...  60.7 us
    pallas_call x1, Pallas kernels, local_kernel(): pl.pallas_call(functools.partial(store, rows // 8), out_shape=(whole, who...  33 us

profile of v5, /device:TPU:0, one launch (start us, length us, event | category | flops | bytes accessed | tf_op | source)
XLA Modules:
  0.0 94.4 jit_solution(15495730325139389287)
XLA Ops:
  0.6 60.7 %shard_map.50 = (bf16[32,16,4,128]{3,2,1,0:T(4,128)(2,1)}, bf16[32,16,4,128]{3,2,1,0:T(4,128)(2,1)}) custom-call(bf16[32,16,4,128]{3,2,1,0:T(4,128)(2,1)} %act_hbm.1, bf16[32,16,4,128]{3,2,1,0:T(4,128)(2,1)} %grad_hbm.1, bf16[27,32,128]{2,1,0:T(8,128)(2,1)} %bitcast.1), custom_call_target="tpu_custom_call" | custom-call | flops 3623878656 | bytes 2097152 | tf_op jit(solution)/shard_map/pallas_call | solution.py:438
  61.4 33.0 %shard_map.51 = (bf16[32,16,4,128]{3,2,1,0:T(4,128)(2,1)}, bf16[32,16,4,128]{3,2,1,0:T(4,128)(2,1)}) custom-call(bf16[32,16,4,128]{3,2,1,0:T(4,128)(2,1)} %get-tuple-element.4.features, bf16[32,16,4,128]{3,2,1,0:T(4,128)(2,1)} %get-tuple-element.5.gradient), custom_call_target="tpu_custom_call" | custom-call | tf_op jit(solution)/shard_map/pallas_call | solution.py:470

commit v6 on v1

--- a/solution.py
+++ b/solution.py
@@ -75,33 +75,41 @@
 
 
 def kernel(
-    dims, act, grad, wsl, outf, outg,
-    xa, xg, gathered, lf, lb, yf, yg,
+    dims, act, grad, weight, outf, outg,
+    wsl, xa, xg, gathered, lf, lb, yf, yg,
     w1_send, w1_recv, w2_send, w2_recv, in_send, in_recv, halo_send, halo_recv,
-    out_send, out_recv, own,
+    out_send, out_recv, extra_send, extra_recv, own,
 ):
     n, m, rows, block, depth, height, taps = dims
     chans = m * rows
-    per = wsl.shape[0]
+    per = -(-taps // n)
     plane = depth * height
     span = block * plane
     g = lax.axis_index("gx")
     d = lax.axis_index("ch")
-
-    def block_of(gg, dd):
-        return jnp.where(lax.rem(gg, 2) == 0, dd, m - 1 - dd)
-
-    k = block_of(g, d)
+    pair, c = lax.div(g, 2), lax.rem(g, 2)
+
+    def level(pp, at):
+        return jnp.where(lax.rem(pp, 2) == 0, at, m - 1 - at)
 
     def device_of(index):
-        gg = lax.div(index, m)
-        return gg, block_of(gg, lax.rem(index, m))
-
+        pp, at = lax.div(index, 2 * m), lax.rem(index, 2 * m)
+        return 2 * pp + lax.rem(at, 2), level(pp, lax.div(at, 2))
+
+    place = 2 * level(pair, d) + c
+    source, k = lax.div(place, m), lax.rem(place, m)
+    holds_own = source == c
     whole = n * m
-    spot = g * m + k
+    spot = pair * 2 * m + place
     prev = device_of(lax.rem(spot + whole - 1, whole))
     following = device_of(lax.rem(spot + 1, whole))
 
+    def worker(q):
+        return device_of(pair * 2 * m + c * m + q)
+
+    def holder(dd):
+        return 2 * pair + source, dd
+
     def rows_at(dd):
         return pl.ds(pl.multiple_of(dd * rows, rows), rows)
 
@@ -109,11 +117,18 @@
         return pl.ds(pl.multiple_of(kk * span, 128), span)
 
     barrier = pltpu.get_barrier_semaphore()
-    for r in range(1, m):
-        pl.semaphore_signal(barrier, inc=1, device_id=(g, lax.rem(d + r, m)), device_id_type=MESH)
-    for r in range(1, n):
-        pl.semaphore_signal(barrier, inc=1, device_id=(lax.rem(g + r, n), d), device_id_type=MESH)
-    pl.semaphore_wait(barrier, m - 1 + n - 1)
+    for side in range(2):
+        for r in range(m):
+            if side + r > 0:
+                pl.semaphore_signal(
+                    barrier, inc=1, device_id_type=MESH,
+                    device_id=(2 * pair + lax.rem(c + side, 2), lax.rem(d + r, m)),
+                )
+    for r in range(2, n):
+        pl.semaphore_signal(
+            barrier, inc=1, device_id=(lax.rem(2 * pair + r, n), d), device_id_type=MESH
+        )
+    pl.semaphore_wait(barrier, 2 * m - 1 + n - 2)
 
     def remote(src, dst, send, recv, where):
         return pltpu.make_async_remote_copy(
@@ -134,14 +149,82 @@
         part = gathered.at[pl.ds(at * per, per), :, :]
         return remote(part, part, w2_send.at[r], w2_recv.at[r], (gg, d))
 
-    def spread(which, x, field, r, sending):
-        dd = lax.rem(d + r, m) if sending else lax.rem(d + m - r, m)
-        at = d if sending else dd
-        return remote(
-            field.at[:, cols_at(block_of(g, dd) if sending else k)],
-            x.at[rows_at(at), pl.ds(plane, span)],
-            in_send.at[which, r], in_recv.at[which, r], (g, dd),
-        )
+    inner = pl.ds(plane, span)
+
+    def spread_out(which, x, field, q):
+        return remote(
+            field.at[:, cols_at(q)], x.at[rows_at(d), inner],
+            in_send.at[which, q], in_recv.at[which, d], worker(q),
+        )
+
+    def spread_in(which, x, field, dd):
+        return remote(
+            field.at[:, cols_at(k)], x.at[rows_at(dd), inner],
+            in_send.at[which, k], in_recv.at[which, dd], holder(dd),
+        )
+
+    def foreign_work(q):
+        return c * m + q != place
+
+    def foreign_holder(dd):
+        return jnp.logical_or(jnp.logical_not(holds_own), dd != d)
+
+    low_end, high_end = pl.ds(0, plane), pl.ds(m * span - plane, plane)
+    low_slot, high_slot = pl.ds(0, plane), pl.ds(span + plane, plane)
+    edges = ((high_end, low_slot, m), (low_end, high_slot, m - 1))
+
+    def extra(which, x, field, side, dd, where):
+        src, dst, _ = edges[side]
+        return remote(
+            field.at[:, src], x.at[rows_at(dd), dst],
+            extra_send.at[which], extra_recv.at[which, dd], where,
+        )
+
+    def extra_each(which, x, field, act_on):
+        for side in range(2):
+            @pl.when(jnp.logical_and(c == side, place != edges[side][2]))
+            def _():
+                act_on(extra(which, x, field, side, d, device_of(pair * 2 * m + edges[side][2])))
+
+    def extra_landed(which, x, field):
+        for side in range(2):
+            @pl.when(place == edges[side][2])
+            def _():
+                for r in range(1, m):
+                    dd = lax.rem(d + r, m)
+                    extra(which, x, field, side, dd, (g, dd)).wait_recv()
+
+    def spread_start(which, x, field, q):
+        @pl.when(foreign_work(q))
+        def _():
+            spread_out(which, x, field, q).start()
+
+    def spread_sent(which, x, field, q):
+        @pl.when(foreign_work(q))
+        def _():
+            spread_out(which, x, field, q).wait_send()
+
+    def spread_landed(which, x, field):
+        for dd in range(m):
+            @pl.when(foreign_holder(dd))
+            def _():
+                spread_in(which, x, field, dd).wait_recv()
+        extra_landed(which, x, field)
+
+    def spread_own(which, x, field):
+        def move(src, dst):
+            copy = pltpu.make_async_copy(field.at[:, src], x.at[rows_at(d), dst], own.at[1 + which])
+            copy.start()
+            copy.wait()
+
+        @pl.when(holds_own)
+        def _():
+            move(cols_at(k), inner)
+
+        for side in range(2):
+            @pl.when(place == edges[side][2])
+            def _():
+                move(edges[side][0], edges[side][1])
 
     def halo(which, x, side):
         first, last = pl.ds(plane, plane), pl.ds(span, plane)
@@ -151,28 +234,88 @@
             x.at[:, src], x.at[:, dst], halo_send.at[which, side], halo_recv.at[which, side], where
         )
 
-    def collect(which, y, out, r, sending):
-        dd = lax.rem(d + r, m) if sending else lax.rem(d + m - r, m)
-        at = k if sending else block_of(g, dd)
-        return remote(
-            y.at[rows_at(dd if sending else d), :], out.at[:, cols_at(at)],
-            out_send.at[which, r], out_recv.at[which, r], (g, dd),
-        )
-
-    own_copies = [
-        pltpu.make_async_copy(wsl, gathered.at[mine, rows_at(d), :], own.at[0]),
-        pltpu.make_async_copy(act.at[:, cols_at(k)], xa.at[rows_at(d), pl.ds(plane, span)], own.at[1]),
-        pltpu.make_async_copy(grad.at[:, cols_at(k)], xg.at[rows_at(d), pl.ds(plane, span)], own.at[2]),
-    ]
+    has_prev, has_next = place != m, place != m - 1
+    sends, lands = (has_prev, has_next), (has_next, has_prev)
+
+    def halo_start(which, x):
+        for side in range(2):
+            @pl.when(sends[side])
+            def _():
+                halo(which, x, side).start()
+
+    def halo_sent(which, x):
+        for side in range(2):
+            @pl.when(sends[side])
+            def _():
+                halo(which, x, side).wait_send()
+
+    def halo_landed(which, x):
+        for side in range(2):
+            @pl.when(lands[side])
+            def _():
+                halo(which, x, side).wait_recv()
+
+    pieces = [(0, plane), ((block - 1) * plane, plane)]
+    if block > 2:
+        pieces.append((plane, (block - 2) * plane))
+
+    def collect_out(which, y, out, j, dd):
+        at, size = pieces[j]
+        return remote(
+            y.at[rows_at(dd), pl.ds(at, size)],
+            out.at[:, pl.ds(pl.multiple_of(k * span + at, 128), size)],
+            out_send.at[which, j, dd], out_recv.at[which, j, k], holder(dd),
+        )
+
+    def collect_in(which, y, out, j, q):
+        at, size = pieces[j]
+        return remote(
+            y.at[rows_at(d), pl.ds(at, size)], out.at[:, pl.ds(q * span + at, size)],
+            out_send.at[which, j, d], out_recv.at[which, j, q], worker(q),
+        )
+
+    def collect_own(which, y, out):
+        return pltpu.make_async_copy(y.at[rows_at(d), :], out.at[:, cols_at(k)], own.at[3 + which])
+
+    def collect_start(which, y, out, parts):
+        for r in range(m):
+            dd = lax.rem(d + r, m)
+
+            @pl.when(foreign_holder(dd))
+            def _():
+                for j in parts:
+                    collect_out(which, y, out, j, dd).start()
+
+    def collect_finish(which, y, out):
+        @pl.when(holds_own)
+        def _():
+            collect_own(which, y, out).wait()
+
+        for q in range(m):
+            @pl.when(foreign_work(q))
+            def _():
+                for j in range(len(pieces)):
+                    collect_in(which, y, out, j, q).wait_recv()
+
+            @pl.when(foreign_holder(q))
+            def _():
+                for j in range(len(pieces)):
+                    collect_out(which, y, out, j, q).wait_send()
+
+    for i in range(per):
+        wsl[i] = weight[jnp.minimum(g * per + i, taps - 1)]
     others, peers = range(1, m), range(1, n)
+    order = [lax.rem(d + r, m) for r in range(m)]
     for r in others:
         w1(r, True).start()
-    for r in others:
-        spread(0, xa, act, r, True).start()
-    for c in own_copies:
-        c.start()
-    for c in own_copies:
-        c.wait()
+    for q in order:
+        spread_start(0, xa, act, q)
+    extra_each(0, xa, act, lambda copy: copy.start())
+    own_filters = pltpu.make_async_copy(wsl, gathered.at[mine, rows_at(d), :], own.at[0])
+    own_filters.start()
+    spread_own(0, xa, act)
+    spread_own(1, xg, grad)
+    own_filters.wait()
     for r in others:
         w1(r, False).wait_recv()
 
@@ -181,27 +324,27 @@
         for r in peers:
             w2(r, True).start()
 
-    for r in others:
-        spread(0, xa, act, r, True).wait_send()
-    for r in others:
-        spread(1, xg, grad, r, True).start()
-    for r in others:
-        spread(0, xa, act, r, False).wait_recv()
-    for side in range(2):
-        halo(0, xa, side).start()
+    for q in order:
+        spread_sent(0, xa, act, q)
+        spread_start(1, xg, grad, q)
+    extra_each(1, xg, grad, lambda copy: copy.start())
+    spread_landed(0, xa, act)
+    halo_start(0, xa)
 
     for r in peers:
         @pl.when(lax.rem(g + n - r, n) * per < taps)
         def _():
             w2(r, False).wait_recv()
 
-    for a in range(3):
-        for b in range(3):
-            for c in range(3):
-                at = pl.ds((3 * c + a) * chans, chans)
-                lf[pl.ds(b * chans, chans), at] = gathered[9 * a + 3 * b + c]
-                lb[pl.ds(b * chans, chans), at] = gathered[9 * (2 - a) + 3 * (2 - b) + 2 - c].T
-
+    def filters(l, backward):
+        for a in range(3):
+            for b in range(3):
+                for e in range(3):
+                    tap = 9 * a + 3 * b + e
+                    part = gathered[taps - 1 - tap].T if backward else gathered[tap]
+                    l[pl.ds(b * chans, chans), pl.ds((3 * e + a) * chans, chans)] = part
+
+    filters(lf, False)
     lane = lax.broadcasted_iota(jnp.int32, (chans, height), 1)
 
     def pair_sum(x, l, y, pair):
@@ -234,34 +377,31 @@
     def finish(which, x, l, y, out):
         for s in range(2, block, 2):
             pair_sum(x, l, y, (s, s + 1))
-        for side in range(2):
-            halo(which, x, side).wait_recv()
+        if block > 2:
+            collect_start(which, y, out, (2,))
+        halo_landed(which, x)
         pair_sum(x, l, y, (1, block))
-        for r in others:
-            collect(which, y, out, r, True).start()
-        copy = pltpu.make_async_copy(y.at[rows_at(d), :], out.at[:, cols_at(k)], own.at[3 + which])
-        copy.start()
-        return copy
-
-    first_own = finish(0, xa, lf, yf, outf)
+        collect_start(which, y, out, (0, 1))
+
+        @pl.when(holds_own)
+        def _():
+            collect_own(which, y, out).start()
+
+    finish(0, xa, lf, yf, outf)
+    filters(lb, True)
+    spread_landed(1, xg, grad)
+    halo_start(1, xg)
+    finish(1, xg, lb, yg, outg)
+
     for r in others:
-        spread(1, xg, grad, r, False).wait_recv()
-    for side in range(2):
-        halo(1, xg, side).start()
-    second_own = finish(1, xg, lb, yg, outg)
-
-    first_own.wait()
-    second_own.wait()
-    for r in others:
-        collect(0, yf, outf, r, False).wait_recv()
-        collect(1, yg, outg, r, False).wait_recv()
         w1(r, True).wait_send()
-        spread(1, xg, grad, r, True).wait_send()
-        collect(0, yf, outf, r, True).wait_send()
-        collect(1, yg, outg, r, True).wait_send()
-    for which, x in ((0, xa), (1, xg)):
-        for side in range(2):
-            halo(which, x, side).wait_send()
+    for q in order:
+        spread_sent(1, xg, grad, q)
+    for which, x, field in ((0, xa, act), (1, xg, grad)):
+        extra_each(which, x, field, lambda copy: copy.wait_send())
+        halo_sent(which, x)
+    collect_finish(0, yf, outf)
+    collect_finish(1, yg, outg)
 
     @pl.when(g * per < taps)
     def _():
@@ -276,9 +416,6 @@
     block = planes // m
     plane = depth * height
     per = -(-taps // n)
-    padded = jnp.pad(conv_weight, ((0, per * n - taps), (0, 0), (0, 0)))
-    wsl = lax.dynamic_slice_in_dim(padded, lax.axis_index("gx") * per, per, axis=0)
-    wsl = jnp.swapaxes(wsl, 1, 2)
     vmem = pl.BlockSpec(memory_space=pltpu.VMEM)
     flat = jax.ShapeDtypeStruct((rows, planes * plane), jnp.bfloat16)
     sem = pltpu.SemaphoreType.DMA
@@ -289,6 +426,7 @@
         in_specs=[vmem] * 3,
         out_specs=(vmem, vmem),
         scratch_shapes=[
+            pltpu.VMEM((per, rows, chans), jnp.bfloat16),
             pltpu.VMEM((chans, (block + 2) * plane), jnp.bfloat16),
             pltpu.VMEM((chans, (block + 2) * plane), jnp.bfloat16),
             pltpu.VMEM((per * n, chans, chans), jnp.bfloat16),
@@ -298,22 +436,22 @@
             pltpu.VMEM((chans, block * plane), jnp.bfloat16),
             sem((m,)), sem((m,)), sem((n,)), sem((n,)),
             sem((2, m)), sem((2, m)), sem((2, 2)), sem((2, 2)),
-            sem((2, m)), sem((2, m)), sem((5,)),
+            sem((2, 3, m)), sem((2, 3, m)), sem((2,)), sem((2, m)), sem((5,)),
         ],
         compiler_params=pltpu.CompilerParams(
-            collective_id=0, has_side_effects=True, vmem_limit_bytes=40 * 2**20
+            collective_id=0, has_side_effects=True, vmem_limit_bytes=20 * 2**20
         ),
         cost_estimate=pl.CostEstimate(
             flops=flops, bytes_accessed=8 * rows * planes * plane, transcendentals=0
         ),
-    )(activations.reshape(rows, -1), out_grad.reshape(rows, -1), wsl)
+    )(activations.reshape(rows, -1), out_grad.reshape(rows, -1), jnp.swapaxes(conv_weight, 1, 2))
     return features.reshape(activations.shape), gradient.reshape(out_grad.shape)
 
 
 def local(activations, conv_weight, out_grad):
     n, m = lax.axis_size("gx"), lax.axis_size("ch")
     rows, planes, _, height = activations.shape
-    fits = rows % 16 == 0 and planes % (2 * m) == 0 and height % 128 == 0 and n % 2 == 0
+    fits = rows % 16 == 0 and planes % (2 * m) == 0 and height % 128 == 0 and n % 4 == 0 and m % 2 == 0
     plan = local_kernel if fits else local_plain
     return plan(activations, conv_weight, out_grad)
 

time: 68.5 us -> 65 us (0.949)
  Pallas kernels: 62.7 us -> 59 us
    pallas_call x1, Pallas kernels: 62.7 us -> 59 us  [local_kernel(): pl.pallas_call(functools.partial(kernel, (n, m, rows, block, depth, heigh...]
    transpose x1 -> x0, local copies, waits for them, and re-layouts: 0.78 us -> none  [local_kernel(): wsl = jnp.swapaxes(wsl, 1, 2)]
where the time goes in v6:
time: 65 us; the launch traced here: 64.4 us
  Pallas kernels  59 us (91%)
  local copies, waits for them, and re-layouts  4.73 us (7%)
  between operations  0.67 us (1%)
    pallas_call x1, Pallas kernels, local_kernel(): pl.pallas_call(functools.partial(kernel, (n, m, rows, block, depth, heigh...  59 us
    reshape x1, local copies, waits for them, and re-layouts, local_kernel(): activations.reshape(rows, -1)  1.48 us

profile of v6, /device:TPU:0, one launch (start us, length us, event | category | flops | bytes accessed | tf_op | source)
XLA Modules:
  0.0 64.4 jit_solution(11522089111746877526)
XLA Ops:
  0.6 0.0 copy-start.1
  0.6 1.5 %reshape.16.act = bf16[32,8192]{1,0:T(8,128)(2,1)S(1)} reshape(bf16[32,16,4,128]{3,2,1,0:T(4,128)(2,1)} %param.3) | data formatting | bytes 1048576 | tf_op jit(solution)/shard_map/reshape | solution.py:447
  2.1 0.0 copy-done.1
  2.1 0.0 copy-start
  2.1 0.4 reshape.17.grad
  2.5 0.5 copy-done
  3.1 59.0 %shard_map.50 = (bf16[32,8192]{1,0:T(8,128)(2,1)S(1)}, bf16[32,8192]{1,0:T(8,128)(2,1)S(1)}) custom-call(bf16[32,8192]{1,0:T(8,128)(2,1)S(1)} %reshape.16.act, bf16[32,8192]{1,0:T(8,128)(2,1)S(1)} %reshape.17.grad, bf16[27,32,128]{2,1,0:T(8,128)(2,1)S(1)} %bitcast.1), custom_call_target="tpu_custom_call" | custom-call | flops 3623878656 | bytes 2097152 | tf_op jit(solution)/shard_map/pallas_call | solution.py:423
  62.1 1.2 %reshape.18 = bf16[32,16,4,128]{3,2,1,0:T(4,128)(2,1)} reshape(bf16[32,8192]{1,0:T(8,128)(2,1)S(1)} %get-tuple-element.4) | data formatting | bytes 1048576 | tf_op jit(solution)/shard_map/reshape | solution.py:448
  63.3 1.2 %reshape.19 = bf16[32,16,4,128]{3,2,1,0:T(4,128)(2,1)} reshape(bf16[32,8192]{1,0:T(8,128)(2,1)S(1)} %get-tuple-element.5) | data formatting | bytes 1048576 | tf_op jit(solution)/shard_map/reshape | solution.py:448
Async XLA Ops:
  0.6 1.5 %copy-start.1 = (bf16[32,16,4,128]{3,2,1,0:T(4,128)(2,1)S(1)}, bf16[32,16,4,128]{3,2,1,0:T(4,128)(2,1)}, u32[]{:S(2)}) copy-start(bf16[32,16,4,128]{3,2,1,0:T(4,128)(2,1)} %param.5) | copy-start | bytes 1572868
  2.1 0.9 %copy-start = (bf16[27,128,32]{1,2,0:T(8,128)(2,1)S(1)}, bf16[27,128,32]{1,2,0:T(8,128)(2,1)}, u32[]{:S(2)}) copy-start(bf16[27,128,32]{1,2,0:T(8,128)(2,1)} %param.4) | copy-start | bytes 663556

commit v7 on v6

--- a/solution.py
+++ b/solution.py
@@ -138,10 +138,22 @@
 
     mine = pl.ds(g * per, per)
 
-    def w1(r, sending):
-        dd = lax.rem(d + r, m) if sending else lax.rem(d + m - r, m)
+    half = m // 2
+    across = lax.rem(d + half, m)
+    base = lax.div(d, half) * half
+
+    def w1(sending):
+        at = rows_at(d if sending else across)
+        return remote(wsl, gathered.at[mine, at, :], w1_send.at[0], w1_recv.at[0], (g, across))
+
+    def w1_share(r, far, sending):
+        dd = base + lax.rem(d - base + (r if sending else half - r), half)
         at = d if sending else dd
-        return remote(wsl, gathered.at[mine, rows_at(at), :], w1_send.at[r], w1_recv.at[r], (g, dd))
+        part = gathered.at[mine, rows_at(lax.rem(at + half, m) if far else at), :]
+        slot = 1 + 2 * (r - 1) + far
+        return remote(part, part, w1_send.at[slot], w1_recv.at[slot], (g, dd))
+
+    shares = [(r, far) for r in range(1, half) for far in range(2)]
 
     def w2(r, sending):
         gg = lax.rem(g + r, n) if sending else lax.rem(g + n - r, n)
@@ -304,20 +316,24 @@
 
     for i in range(per):
         wsl[i] = weight[jnp.minimum(g * per + i, taps - 1)]
-    others, peers = range(1, m), range(1, n)
+    peers = range(1, n)
     order = [lax.rem(d + r, m) for r in range(m)]
-    for r in others:
-        w1(r, True).start()
+    w1(True).start()
     for q in order:
         spread_start(0, xa, act, q)
     extra_each(0, xa, act, lambda copy: copy.start())
     own_filters = pltpu.make_async_copy(wsl, gathered.at[mine, rows_at(d), :], own.at[0])
     own_filters.start()
+    own_filters.wait()
+    for r in range(1, half):
+        w1_share(r, 0, True).start()
     spread_own(0, xa, act)
     spread_own(1, xg, grad)
-    own_filters.wait()
-    for r in others:
-        w1(r, False).wait_recv()
+    w1(False).wait_recv()
+    for r in range(1, half):
+        w1_share(r, 1, True).start()
+    for r, far in shares:
+        w1_share(r, far, False).wait_recv()
 
     @pl.when(g * per < taps)
     def _():
@@ -393,8 +409,9 @@
     halo_start(1, xg)
     finish(1, xg, lb, yg, outg)
 
-    for r in others:
-        w1(r, True).wait_send()
+    w1(True).wait_send()
+    for r, far in shares:
+        w1_share(r, far, True).wait_send()
     for q in order:
         spread_sent(1, xg, grad, q)
     for which, x, field in ((0, xa, act), (1, xg, grad)):

time: 65 us -> 63.6 us (0.978)
  Pallas kernels: 59 us -> 57.7 us
    pallas_call x1, Pallas kernels: 59 us -> 57.7 us  [local_kernel(): pl.pallas_call(functools.partial(kernel, (n, m, rows, block, depth, heigh...]
where the time goes in v7:
time: 63.6 us; the launch traced here: 63.1 us
  Pallas kernels  57.7 us (91%)
  local copies, waits for them, and re-layouts  4.73 us (7%)
  between operations  0.67 us (1%)
    pallas_call x1, Pallas kernels, local_kernel(): pl.pallas_call(functools.partial(kernel, (n, m, rows, block, depth, heigh...  57.7 us
    reshape x1, local copies, waits for them, and re-layouts, local_kernel(): activations.reshape(rows, -1)  1.48 us

profile of v7, /device:TPU:0, one launch (start us, length us, event | category | flops | bytes accessed | tf_op | source)
XLA Modules:
  0.0 63.1 jit_solution(15898200046150339106)
XLA Ops:
  0.6 0.0 copy-start.1
  0.6 1.5 %reshape.16.act = bf16[32,8192]{1,0:T(8,128)(2,1)S(1)} reshape(bf16[32,16,4,128]{3,2,1,0:T(4,128)(2,1)} %param.3) | data formatting | bytes 1048576 | tf_op jit(solution)/shard_map/reshape | solution.py:464
  2.1 0.0 copy-done.1
  2.1 0.0 copy-start
  2.1 0.4 reshape.17.grad
  2.5 0.5 copy-done
  3.1 57.7 %shard_map.50 = (bf16[32,8192]{1,0:T(8,128)(2,1)S(1)}, bf16[32,8192]{1,0:T(8,128)(2,1)S(1)}) custom-call(bf16[32,8192]{1,0:T(8,128)(2,1)S(1)} %reshape.16.act, bf16[32,8192]{1,0:T(8,128)(2,1)S(1)} %reshape.17.grad, bf16[27,32,128]{2,1,0:T(8,128)(2,1)S(1)} %bitcast.1), custom_call_target="tpu_custom_call" | custom-call | flops 3623878656 | bytes 2097152 | tf_op jit(solution)/shard_map/pallas_call | solution.py:440
  60.7 1.2 %reshape.18 = bf16[32,16,4,128]{3,2,1,0:T(4,128)(2,1)} reshape(bf16[32,8192]{1,0:T(8,128)(2,1)S(1)} %get-tuple-element.4) | data formatting | bytes 1048576 | tf_op jit(solution)/shard_map/reshape | solution.py:465
  61.9 1.2 %reshape.19 = bf16[32,16,4,128]{3,2,1,0:T(4,128)(2,1)} reshape(bf16[32,8192]{1,0:T(8,128)(2,1)S(1)} %get-tuple-element.5) | data formatting | bytes 1048576 | tf_op jit(solution)/shard_map/reshape | solution.py:465
Async XLA Ops:
  0.6 1.5 %copy-start.1 = (bf16[32,16,4,128]{3,2,1,0:T(4,128)(2,1)S(1)}, bf16[32,16,4,128]{3,2,1,0:T(4,128)(2,1)}, u32[]{:S(2)}) copy-start(bf16[32,16,4,128]{3,2,1,0:T(4,128)(2,1)} %param.5) | copy-start | bytes 1572868
  2.1 0.9 %copy-start = (bf16[27,128,32]{1,2,0:T(8,128)(2,1)S(1)}, bf16[27,128,32]{1,2,0:T(8,128)(2,1)}, u32[]{:S(2)}) copy-start(bf16[27,128,32]{1,2,0:T(8,128)(2,1)} %param.4) | copy-start | bytes 663556

commit v8 on v7

--- a/solution.py
+++ b/solution.py
@@ -155,11 +155,23 @@
 
     shares = [(r, far) for r in range(1, half) for far in range(2)]
 
+    sibling = 2 * pair + 1 - c
+
+    def slab(at):
+        return gathered.at[pl.ds(at * per, per), :, :]
+
+    def full(at):
+        return at * per < taps
+
     def w2(r, sending):
         gg = lax.rem(g + r, n) if sending else lax.rem(g + n - r, n)
-        at = g if sending else gg
-        part = gathered.at[pl.ds(at * per, per), :, :]
+        part = slab(g if sending else gg)
         return remote(part, part, w2_send.at[r], w2_recv.at[r], (gg, d))
+
+    def pass_on(r, sending):
+        at = lax.rem((g if sending else sibling) + n - r, n)
+        copy = remote(slab(at), slab(at), w2_send.at[r + 1], w2_recv.at[r + 1], (sibling, d))
+        return full(at), copy
 
     inner = pl.ds(plane, span)
 
@@ -316,7 +328,6 @@
 
     for i in range(per):
         wsl[i] = weight[jnp.minimum(g * per + i, taps - 1)]
-    peers = range(1, n)
     order = [lax.rem(d + r, m) for r in range(m)]
     w1(True).start()
     for q in order:
@@ -335,10 +346,19 @@
     for r, far in shares:
         w1_share(r, far, False).wait_recv()
 
-    @pl.when(g * per < taps)
+    steps = range(2, n, 2)
+
+    @pl.when(full(g))
     def _():
-        for r in peers:
+        for r in steps:
             w2(r, True).start()
+        pass_on(0, True)[1].start()
+
+    for r in steps:
+        @pl.when(full(lax.rem(g + n - r, n)))
+        def _():
+            w2(r, False).wait_recv()
+            pass_on(r, True)[1].start()
 
     for q in order:
         spread_sent(0, xa, act, q)
@@ -347,10 +367,12 @@
     spread_landed(0, xa, act)
     halo_start(0, xa)
 
-    for r in peers:
-        @pl.when(lax.rem(g + n - r, n) * per < taps)
-        def _():
-            w2(r, False).wait_recv()
+    for r in range(0, n, 2):
+        here, copy = pass_on(r, False)
+
+        @pl.when(here)
+        def _():
+            copy.wait_recv()
 
     def filters(l, backward):
         for a in range(3):
@@ -420,10 +442,17 @@
     collect_finish(0, yf, outf)
     collect_finish(1, yg, outg)
 
-    @pl.when(g * per < taps)
+    @pl.when(full(g))
     def _():
-        for r in peers:
+        for r in steps:
             w2(r, True).wait_send()
+
+    for r in range(0, n, 2):
+        here, copy = pass_on(r, True)
+
+        @pl.when(here)
+        def _():
+            copy.wait_send()
 
 
 def local_kernel(activations, conv_weight, out_grad):

time: 63.6 us -> 65.1 us (1.024)
  the two profiles are of different devices: /device:TPU:0 before, /device:TPU:28 now
where the time goes in v8:
time: 65.1 us; the launch traced here: 65 us
  Pallas kernels  59.6 us (92%)
  local copies, waits for them, and re-layouts  4.73 us (7%)
  between operations  0.67 us (1%)
    pallas_call x1, Pallas kernels, local_kernel(): pl.pallas_call(functools.partial(kernel, (n, m, rows, block, depth, heigh...  59.6 us
    reshape x1, local copies, waits for them, and re-layouts, local_kernel(): activations.reshape(rows, -1)  1.48 us

profile of v8, /device:TPU:28, one launch (start us, length us, event | category | flops | bytes accessed | tf_op | source)
XLA Modules:
  0.0 65.0 jit_solution(15822849175946661663)
XLA Ops:
  0.6 0.0 copy-start.1
  0.6 1.5 %reshape.16.act = bf16[32,8192]{1,0:T(8,128)(2,1)S(1)} reshape(bf16[32,16,4,128]{3,2,1,0:T(4,128)(2,1)} %param.3) | data formatting | bytes 1048576 | tf_op jit(solution)/shard_map/reshape | solution.py:493
  2.1 0.0 copy-done.1
  2.1 0.0 copy-start
  2.1 0.4 reshape.17.grad
  2.5 0.5 copy-done
  3.1 59.6 %shard_map.50 = (bf16[32,8192]{1,0:T(8,128)(2,1)S(1)}, bf16[32,8192]{1,0:T(8,128)(2,1)S(1)}) custom-call(bf16[32,8192]{1,0:T(8,128)(2,1)S(1)} %reshape.16.act, bf16[32,8192]{1,0:T(8,128)(2,1)S(1)} %reshape.17.grad, bf16[27,32,128]{2,1,0:T(8,128)(2,1)S(1)} %bitcast.1), custom_call_target="tpu_custom_call" | custom-call | flops 3623878656 | bytes 2097152 | tf_op jit(solution)/shard_map/pallas_call | solution.py:469
  62.7 1.2 %reshape.18 = bf16[32,16,4,128]{3,2,1,0:T(4,128)(2,1)} reshape(bf16[32,8192]{1,0:T(8,128)(2,1)S(1)} %get-tuple-element.4) | data formatting | bytes 1048576 | tf_op jit(solution)/shard_map/reshape | solution.py:494
  63.8 1.2 %reshape.19 = bf16[32,16,4,128]{3,2,1,0:T(4,128)(2,1)} reshape(bf16[32,8192]{1,0:T(8,128)(2,1)S(1)} %get-tuple-element.5) | data formatting | bytes 1048576 | tf_op jit(solution)/shard_map/reshape | solution.py:494
Async XLA Ops:
  0.6 1.5 %copy-start.1 = (bf16[32,16,4,128]{3,2,1,0:T(4,128)(2,1)S(1)}, bf16[32,16,4,128]{3,2,1,0:T(4,128)(2,1)}, u32[]{:S(2)}) copy-start(bf16[32,16,4,128]{3,2,1,0:T(4,128)(2,1)} %param.5) | copy-start | bytes 1572868
  2.1 0.9 %copy-start = (bf16[27,128,32]{1,2,0:T(8,128)(2,1)S(1)}, bf16[27,128,32]{1,2,0:T(8,128)(2,1)}, u32[]{:S(2)}) copy-start(bf16[27,128,32]{1,2,0:T(8,128)(2,1)} %param.4) | copy-start | bytes 663556

commit v9 on v7

--- a/solution.py
+++ b/solution.py
@@ -322,6 +322,9 @@
     for q in order:
         spread_start(0, xa, act, q)
     extra_each(0, xa, act, lambda copy: copy.start())
+    for q in order:
+        spread_start(1, xg, grad, q)
+    extra_each(1, xg, grad, lambda copy: copy.start())
     own_filters = pltpu.make_async_copy(wsl, gathered.at[mine, rows_at(d), :], own.at[0])
     own_filters.start()
     own_filters.wait()
@@ -342,8 +345,6 @@
 
     for q in order:
         spread_sent(0, xa, act, q)
-        spread_start(1, xg, grad, q)
-    extra_each(1, xg, grad, lambda copy: copy.start())
     spread_landed(0, xa, act)
     halo_start(0, xa)
 

time: 63.6 us -> 61.3 us (0.964)
  the two profiles are of different devices: /device:TPU:0 before, /device:TPU:1 now
where the time goes in v9:
time: 61.3 us; the launch traced here: 61.1 us
  Pallas kernels  55.7 us (91%)
  local copies, waits for them, and re-layouts  4.73 us (8%)
  between operations  0.67 us (1%)
    pallas_call x1, Pallas kernels, local_kernel(): pl.pallas_call(functools.partial(kernel, (n, m, rows, block, depth, heigh...  55.7 us
    reshape x1, local copies, waits for them, and re-layouts, local_kernel(): activations.reshape(rows, -1)  1.48 us

profile of v9, /device:TPU:1, one launch (start us, length us, event | category | flops | bytes accessed | tf_op | source)
XLA Modules:
  0.0 61.1 jit_solution(4344157727614317654)
XLA Ops:
  0.6 0.0 copy-start.1
  0.6 1.5 %reshape.16.act = bf16[32,8192]{1,0:T(8,128)(2,1)S(1)} reshape(bf16[32,16,4,128]{3,2,1,0:T(4,128)(2,1)} %param.3) | data formatting | bytes 1048576 | tf_op jit(solution)/shard_map/reshape | solution.py:465
  2.1 0.0 copy-done.1
  2.1 0.0 copy-start
  2.1 0.4 reshape.17.grad
  2.5 0.5 copy-done
  3.1 55.7 %shard_map.50 = (bf16[32,8192]{1,0:T(8,128)(2,1)S(1)}, bf16[32,8192]{1,0:T(8,128)(2,1)S(1)}) custom-call(bf16[32,8192]{1,0:T(8,128)(2,1)S(1)} %reshape.16.act, bf16[32,8192]{1,0:T(8,128)(2,1)S(1)} %reshape.17.grad, bf16[27,32,128]{2,1,0:T(8,128)(2,1)S(1)} %bitcast.1), custom_call_target="tpu_custom_call" | custom-call | flops 3623878656 | bytes 2097152 | tf_op jit(solution)/shard_map/pallas_call | solution.py:441
  58.8 1.2 %reshape.18 = bf16[32,16,4,128]{3,2,1,0:T(4,128)(2,1)} reshape(bf16[32,8192]{1,0:T(8,128)(2,1)S(1)} %get-tuple-element.4) | data formatting | bytes 1048576 | tf_op jit(solution)/shard_map/reshape | solution.py:466
  59.9 1.2 %reshape.19 = bf16[32,16,4,128]{3,2,1,0:T(4,128)(2,1)} reshape(bf16[32,8192]{1,0:T(8,128)(2,1)S(1)} %get-tuple-element.5) | data formatting | bytes 1048576 | tf_op jit(solution)/shard_map/reshape | solution.py:466
Async XLA Ops:
  0.6 1.5 %copy-start.1 = (bf16[32,16,4,128]{3,2,1,0:T(4,128)(2,1)S(1)}, bf16[32,16,4,128]{3,2,1,0:T(4,128)(2,1)}, u32[]{:S(2)}) copy-start(bf16[32,16,4,128]{3,2,1,0:T(4,128)(2,1)} %param.5) | copy-start | bytes 1572868
  2.1 0.9 %copy-start = (bf16[27,128,32]{1,2,0:T(8,128)(2,1)S(1)}, bf16[27,128,32]{1,2,0:T(8,128)(2,1)}, u32[]{:S(2)}) copy-start(bf16[27,128,32]{1,2,0:T(8,128)(2,1)} %param.4) | copy-start | bytes 663556
